TPU v7x, 32 devices: a whole 2x2x4 slice. The times are simulated.
32 devices in a mesh: ty: 4 (over y, core), tx: 8 (over z, x).
Axes of the slice: x: 2, y: 2, z: 4, core: 2. Of those that a mesh axis runs over, the one named last changes fastest.
Arguments:
- covariates: bfloat16 [65536, 512], P(('ty', 'tx')), may hold values from -6 to 6
- w_in: bfloat16 [512, 2048], replicated, may hold values from -0.25 to 0.25
- b_in: float32 [2048], replicated, may hold values from -3 to 3
- w_out: bfloat16 [2048, 128], replicated, may hold values from -0.125 to 0.125
- b_out: float32 [128], replicated, may hold values from -2 to 2
- owner: int32 [65536, 1], P(('ty', 'tx')), may hold values from 0 to 31; in each aligned block of 2048 rows (0 to 2047, 2048 to 4095, ...) at most 128 rows name the same one
- land_cell: int32 [65536], P(('ty', 'tx')), may hold values from 0 to 2047
- row_taps: float32 [128, 9], replicated, may hold values from 0.2 to 1
- col_taps: float32 [128, 9], replicated, may hold values from 0.2 to 1
- rate: float32 [128], replicated, may hold values from 0.2 to 1.5
- capacity: float32 [128], replicated, may hold values from 0.5 to 4
- observed: int32 [64, 1024, 128], P('ty', 'tx'), may hold values from 0 to 2
- surveyed: int32 [64, 1024], P('ty', 'tx'), may hold values 0 or 1
Outputs:
- density: float32 [64, 1024, 128], P('ty', 'tx')
- grad_w_in: float32 [512, 2048], P(('ty', 'tx'))
- grad_w_out: float32 [2048, 128], P(('ty', 'tx'))
Inputs may be any that keep to these rules, and one draw needn't show every extreme that they name: `owner`: among the land cells of one device, no tile owns more than 128, and some tile owns exactly 128.
All inputs are finite; a program needn't handle non-finite values. No bound on the sum of `surveyed` on one device may be relied on, other than what follows from the above.
Results may differ from a plain program's by a relative error of at most 0.0017.
Values may be sent and summed in bfloat16 or wider, within the bound.
A program may use at most 128 MiB of HBM per device.

v0:
```python
import math

import jax
import jax.numpy as jnp
from jax import lax
from jax.sharding import PartitionSpec as P

STEPS = 4


def with_halo(cells, sides, width):
    for axis, dim in sides:
        count = lax.axis_size(axis)
        ends = count - 1
        head = lax.slice_in_dim(cells, 0, width, axis=dim)
        tail = lax.slice_in_dim(cells, cells.shape[dim] - width, cells.shape[dim], axis=dim)
        cells = jnp.concatenate(
            [
                lax.ppermute(tail, axis, [(i, (i + 1) % count) for i in range(ends)]),
                cells,
                lax.ppermute(head, axis, [((i + 1) % count, i) for i in range(ends)]),
            ],
            axis=dim,
        )
    return cells


def normalize(taps):
    return taps / jnp.sum(taps, axis=1, keepdims=True)


def disperse_valid(padded, taps_y, taps_x):
    height = padded.shape[0] - 8
    width_out = padded.shape[1] - 8
    partial_rows = taps_y[:, 0] * padded[0:height]
    for offset in range(1, 9):
        partial_rows = partial_rows + taps_y[:, offset] * padded[offset : offset + height]
    result = taps_x[:, 0] * partial_rows[:, 0:width_out]
    for offset in range(1, 9):
        result = result + taps_x[:, offset] * partial_rows[:, offset : offset + width_out]
    return result


def silu_slope(value):
    sigmoid_v = jax.nn.sigmoid(value)
    return sigmoid_v + value * sigmoid_v * (1.0 - sigmoid_v)


def local(
    covariates,
    w_in,
    b_in,
    w_out,
    b_out,
    owner,
    land_cell,
    row_taps,
    col_taps,
    rate,
    capacity,
    observed,
    surveyed,
):
    row_count = covariates.shape[0]
    tiles_y = lax.axis_size("ty")
    tiles_x = lax.axis_size("tx")
    devices = tiles_y * tiles_x
    slot_count = 2 * row_count // devices
    height, tile_width, species = observed.shape
    cell_count = height * tile_width
    preact = jnp.dot(covariates, w_in, preferred_element_type=jnp.float32) + b_in
    hidden = jax.nn.silu(preact).astype(jnp.bfloat16)
    log_rate = jnp.dot(hidden, w_out, preferred_element_type=jnp.float32) + b_out
    intensity = jnp.exp(log_rate)
    sent = intensity.astype(jnp.bfloat16)
    owner_rows = owner[:, 0]
    onehot = (owner_rows[:, None] == jnp.arange(devices, dtype=jnp.int32)[None, :]).astype(
        jnp.int32
    )
    before = jnp.cumsum(onehot, axis=0) - onehot
    slot_idx = jnp.sum(before * onehot, axis=1)
    flat_slot = owner_rows * slot_count + slot_idx
    send_values = jnp.zeros((devices * slot_count, species), jnp.bfloat16).at[flat_slot].set(sent)
    send_cells = (
        jnp.full((devices * slot_count,), cell_count, jnp.int32).at[flat_slot].set(land_cell)
    )
    got_values, got_cells = (
        lax.all_to_all(
            send_values.reshape(devices, slot_count, species),
            ("ty", "tx"),
            split_axis=0,
            concat_axis=0,
            tiled=True,
        ),
        lax.all_to_all(
            send_cells.reshape(devices, slot_count),
            ("ty", "tx"),
            split_axis=0,
            concat_axis=0,
            tiled=True,
        ),
    )
    cell_list = got_cells.reshape(-1)
    start_field = (
        jnp.zeros((cell_count, species), jnp.float32)
        .at[cell_list]
        .add(got_values.reshape(-1, species).astype(jnp.float32), mode="drop")
    )
    field = 0.1 + start_field.reshape(height, tile_width, species)
    taps_y = normalize(row_taps)
    taps_x = normalize(col_taps)
    back_y = taps_y[:, ::-1]
    back_x = taps_x[:, ::-1]
    scale = 1.0 / math.sqrt(row_count * devices)
    stored = []
    for step in range(STEPS):
        padded = with_halo(field, (("ty", 0), ("tx", 1)), 4)
        mid_value = disperse_valid(padded, taps_y, taps_x)
        stored.append(mid_value)
        field = mid_value * (1.0 + rate) / (1.0 + rate * mid_value / capacity)
    grad_field = (
        surveyed[:, :, None].astype(jnp.float32)
        * (1.0 - observed.astype(jnp.float32) / field)
        * scale
    )
    for step in range(STEPS - 1, -1, -1):
        mid_value = stored[step]
        denom = 1.0 + rate * mid_value / capacity
        grad_mid = grad_field * (1.0 + rate) / (denom * denom)
        padded = with_halo(grad_mid.astype(jnp.bfloat16), (("ty", 0), ("tx", 1)), 4).astype(
            grad_mid.dtype
        )
        grad_field = disperse_valid(padded, back_y, back_x)
    back_values = jnp.take(
        grad_field.reshape(cell_count, species), cell_list, axis=0, mode="fill", fill_value=0.0
    ).astype(jnp.bfloat16)
    home_values = lax.all_to_all(
        back_values.reshape(devices, slot_count, species),
        ("ty", "tx"),
        split_axis=0,
        concat_axis=0,
        tiled=True,
    )
    returned = home_values.reshape(devices * slot_count, species)[flat_slot]
    dlog = (returned.astype(jnp.float32) * intensity).astype(jnp.bfloat16)
    dhidden = lax.dot_general(
        dlog, w_out, (((1,), (1,)), ((), ())), preferred_element_type=jnp.float32
    )
    dpre = (dhidden * silu_slope(preact)).astype(jnp.bfloat16)
    piece = covariates
    grad_w_in = lax.psum_scatter(
        lax.dot_general(piece, dpre, (((0,), (0,)), ((), ())), preferred_element_type=jnp.float32),
        ("ty", "tx"),
        scatter_dimension=0,
        tiled=True,
    )
    piece = hidden
    grad_w_out = lax.psum_scatter(
        lax.dot_general(piece, dlog, (((0,), (0,)), ((), ())), preferred_element_type=jnp.float32),
        ("ty", "tx"),
        scatter_dimension=0,
        tiled=True,
    )
    return (field, grad_w_in, grad_w_out)


def solution(mesh):
    in_specs = (
        P(("ty", "tx"), None),
        P(),
        P(),
        P(),
        P(),
        P(("ty", "tx"), None),
        P(("ty", "tx")),
        P(),
        P(),
        P(),
        P(),
        P("ty", "tx", None),
        P("ty", "tx"),
    )
    out_specs = (P("ty", "tx", None), P(("ty", "tx"), None), P(("ty", "tx"), None))
    return jax.shard_map(local, mesh=mesh, in_specs=in_specs, out_specs=out_specs, check_vma=False)
```

profile of v0, /device:TPU:0, one launch (start us, length us, event | category | flops | bytes accessed | tf_op | source)
XLA Modules:
  0.0 622.9 jit_solution(16702388985078694556)
XLA Ops:
  8.1 9.1 %reduce-window.6 = s32[32,16,128]{2,1,0:T(8,128)S(1)} reduce-window(s32[32,16,128]{2,1,0:T(8,128)S(1)} %fusion.148, s32[]{:T(128)} %constant.14.clone.1), window={size=1x1x128 pad=0_0x0_0x127_0}, to_apply=%region_2.3 | reduce-window | flops 8323072 | bytes 524292 | tf_op jit(solution)/shard_map/reduce-window
  18.0 8.8 %scatter_custom_fusion = s32[4096]{0:T(1024)} fusion(s32[2048]{0:T(1024)S(1)} %bitcast.103, s32[2048]{0:T(1024)} %param.19, s32[]{:T(128)} %constant.12.clone.1), kind=kCustom, calls=%fused_computation.355 | custom fusion | bytes 16896 | tf_op jit(solution)/shard_map/scatter | solution.py:85
  26.8 7.3 %all-to-all-start = ((s32[32,1,128]{2,1,0:T(1,128)}), s32[32,1,128]{2,1,0:T(1,128)S(1)}, u32[]{:S(2)}, u32[]{:S(2)}) async-start(s32[32,1,128]{2,1,0:T(1,128)} %bitcast.9), calls=%async_computation | async-start | bytes 32768 | tf_op jit(solution)/shard_map/all_to_all | solution.py:95
  34.2 10.9 %fusion = (bf16[2048,2048]{1,0:T(8,128)(2,1)S(1)}, f32[2048,2048]{1,0:T(8,128)}) fusion(f32[2048]{0:T(1024)S(1)} %copy-done.13, bf16[2048,512]{1,0:T(8,128)(2,1)S(1)} %copy-done, bf16[512,2048]{1,0:T(8,128)(2,1)} %param.14), kind=kOutput, calls=%fused_computation.8 | convolution fusion | flops 4320133120 | bytes 29368320 | tf_op jit(solution)/shard_map/dot_general | solution.py:71
  50.7 6.8 %scatter_custom_fusion.1 = bf16[4096,128]{1,0:T(8,128)(2,1)} fusion(s32[2048]{0:T(1024)S(1)} %bitcast.104, f32[2048,128]{1,0:T(8,128)S(1)} %fusion.1, bf16[]{:T(256)} %constant.18.clone.1), kind=kCustom, calls=%fused_computation.314 | custom fusion | flops 262144 | bytes 2097154 | tf_op jit(solution)/shard_map/scatter | solution.py:83
  57.5 6.0 all-to-all-start.1
  63.6 27.5 %all-to-all-done.1 = bf16[32,128,128]{2,1,0:T(8,128)(2,1)} async-done(((bf16[32,128,128]{2,1,0:T(8,128)(2,1)}), bf16[32,128,128]{2,1,0:T(8,128)(2,1)}, u32[]{:S(2)}, u32[]{:S(2)}) %all-to-all-start.1) | async-done | bytes 1048608 | tf_op jit(solution)/shard_map/all_to_all | solution.py:88
  91.1 23.0 %scatter_custom_fusion.2 = f32[2048,128]{1,0:T(8,128)S(1)} fusion(s32[4096]{0:T(1024)S(1)} %bitcast.100, bf16[4096,128]{1,0:T(8,128)(2,1)} %bitcast.39, f32[]{:T(128)} %constant.11.clone.1), kind=kCustom, calls=%fused_computation.12 | custom fusion | flops 1048576 | bytes 2097156 | tf_op jit(solution)/shard_map/scatter-add | solution.py:107
  123.9 4.3 collective-permute-done.3
  135.7 5.5 collective-permute-done.5
  146.9 4.3 collective-permute-done.7
  153.3 5.2 collective-permute-start.8
  173.6 5.2 collective-permute-start.12
  195.7 5.2 collective-permute-start.16
  216.6 4.5 collective-permute-start.20
  225.0 4.8 collective-permute-start.22
  275.3 14.9 %gather_fusion = bf16[4096,128]{1,0:T(8,128)(2,1)} fusion(bf16[2048,128]{1,0:T(8,128)(2,1)S(1)} %bitcast.86, s32[4096]{0:T(1024)S(1)} %broadcast_clamp_fusion), kind=kCustom, calls=%fused_computation | custom fusion | bytes 2113536 | tf_op jit(solution)/shard_map/jit(_take)/gather | solution.py:134
  296.9 27.5 %all-to-all-done.2 = bf16[32,128,128]{2,1,0:T(8,128)(2,1)S(1)} async-done(((bf16[32,128,128]{2,1,0:T(8,128)(2,1)}), bf16[32,128,128]{2,1,0:T(8,128)(2,1)S(1)}, u32[]{:S(2)}, u32[]{:S(2)}) %all-to-all-start.2) | async-done | bytes 1048608 | tf_op jit(solution)/shard_map/all_to_all | solution.py:137
  324.4 8.0 %gather_fusion.1 = bf16[2048,128]{1,0:T(8,128)(2,1)} fusion(bf16[4096,128]{1,0:T(8,128)(2,1)S(1)} %bitcast.87, s32[2048]{0:T(1024)S(1)} %broadcast_clamp_fusion.1), kind=kCustom, calls=%fused_computation.1 | custom fusion | bytes 1056768 | tf_op jit(solution)/shard_map/gather | solution.py:144
  332.3 7.2 %fusion.152 = f32[2048,128]{1,0:T(8,128)} fusion(bf16[2048,2048]{1,0:T(8,128)(2,1)} %copy-done.1, f32[2048,128]{1,0:T(8,128)} %copy-done.2, bf16[2048,128]{1,0:T(8,128)(2,1)} %gather_fusion.1), kind=kOutput, calls=%fused_computation.381 | convolution fusion | flops 1074528256 | bytes 11010048 | tf_op jit(solution)/shard_map/dot_general | solution.py:159
  339.9 18.4 %convolution_bitcast_fusion = f32[512,2048]{0,1:T(8,128)} fusion(bf16[2048,512]{1,0:T(8,128)(2,1)S(1)} %copy-done, f32[2048,2048]{1,0:T(8,128)} %get-tuple-element.73, bf16[2048,128]{1,0:T(8,128)(2,1)} %param.16, f32[2048]{0:T(1024)S(1)} %copy-done.13, f32[2048,128]{1,0:T(8,128)S(1)} %copy-done.3, bf16[2048,128]{1,0:T(8,128)(2,1)} %gather_fusion.1), kind=kOutput, calls=%fused_computation.9 | convolution fusion | flops 5411438592 | bytes 25174016 | tf_op jit(solution)/shard_map/dot_general | solution.py:152
  358.3 5.4 copy.24
  366.1 106.3 %reduce-scatter.5.cloned.1.call-done = f32[64,128]{1,0:T(8,128)} async-done(((f32[2048,128]{1,0:T(8,128)}), f32[64,128]{1,0:T(8,128)}) %reduce-scatter.5.cloned.1.call-update) | async-done | bytes 32784 | tf_op jit(solution)/shard_map/reduce_scatter | solution.py:158
  472.4 143.2 %reduce-scatter.7.cloned.1.call-done = f32[16,2048]{1,0:T(8,128)} async-done(((f32[512,2048]{1,0:T(8,128)}), f32[16,2048]{1,0:T(8,128)}) %reduce-scatter.7.cloned.1.call-update) | async-done | bytes 131088
  (154 shorter events, 138.4 us)
Async XLA Ops:
  26.8 30.7 %all-to-all-start = ((s32[32,1,128]{2,1,0:T(1,128)}), s32[32,1,128]{2,1,0:T(1,128)S(1)}, u32[]{:S(2)}, u32[]{:S(2)}) async-start(s32[32,1,128]{2,1,0:T(1,128)} %bitcast.9), calls=%async_computation | async-start | bytes 32768 | tf_op jit(solution)/shard_map/all_to_all | solution.py:95
  57.5 33.5 %all-to-all-start.1 = ((bf16[32,128,128]{2,1,0:T(8,128)(2,1)}), bf16[32,128,128]{2,1,0:T(8,128)(2,1)}, u32[]{:S(2)}, u32[]{:S(2)}) async-start(bf16[32,128,128]{2,1,0:T(8,128)(2,1)} %bitcast.91), calls=%async_computation.1 | async-start | bytes 2097152 | tf_op jit(solution)/shard_map/all_to_all | solution.py:88
  122.2 6.0 collective-permute-start.3
  130.3 5.4 collective-permute-start.4
  134.4 6.8 %collective-permute-start.5 = (f32[4,128,128]{2,1,0:T(8,128)S(1)}, f32[4,128,128]{2,1,0:T(8,128)S(1)}, u32[]{:S(2)}, u32[]{:S(2)}) collective-permute-start(f32[4,128,128]{2,1,0:T(8,128)S(1)} %get-tuple-element.33), channel_id=1, source_target_pairs={{8,0},{16,8},{24,16},{9,1},{17,9},{25,17},{10,2},{18,10},{26,18},{... | collective-permute-start | bytes 786440 | tf_op jit(solution)/shard_map/ppermute | solution.py:21
  141.2 5.7 collective-permute-start.6
  145.2 6.0 collective-permute-start.7
  153.3 6.6 %collective-permute-start.8 = (f32[4,128,128]{2,1,0:T(8,128)S(1)}, f32[4,128,128]{2,1,0:T(8,128)S(1)}, u32[]{:S(2)}, u32[]{:S(2)}) collective-permute-start(f32[4,128,128]{2,1,0:T(8,128)S(1)} %get-tuple-element.30), channel_id=1, source_target_pairs={{0,8},{8,16},{16,24},{1,9},{9,17},{17,25},{2,10},{10,18},{18,26},{... | collective-permute-start | bytes 786440 | tf_op jit(solution)/shard_map/ppermute | solution.py:19
  165.6 6.0 collective-permute-start.11
  173.6 6.6 %collective-permute-start.12 = (f32[4,128,128]{2,1,0:T(8,128)S(1)}, f32[4,128,128]{2,1,0:T(8,128)S(1)}, u32[]{:S(2)}, u32[]{:S(2)}) collective-permute-start(f32[4,128,128]{2,1,0:T(8,128)S(1)} %get-tuple-element.28), channel_id=1, source_target_pairs={{0,8},{8,16},{16,24},{1,9},{9,17},{17,25},{2,10},{10,18},{18,26},{... | collective-permute-start | bytes 786440 | tf_op jit(solution)/shard_map/ppermute | solution.py:19
  185.9 6.0 collective-permute-start.15
  195.7 6.6 %collective-permute-start.16 = (bf16[4,128,128]{2,1,0:T(8,128)(2,1)S(1)}, bf16[4,128,128]{2,1,0:T(8,128)(2,1)S(1)}, u32[]{:S(2)}, u32[]{:S(2)}) collective-permute-start(bf16[4,128,128]{2,1,0:T(8,128)(2,1)S(1)} %get-tuple-element.50), channel_id=1, source_target_pairs={{0,8},{8,16},{16,24},{1,9},{9,17},{17,25},{2,10},{10,18},{18,26},{... | collective-permute-start | bytes 393224 | tf_op jit(solution)/shard_map/ppermute | solution.py:19
  205.0 5.1 collective-permute-start.18
  208.6 5.7 collective-permute-start.19
  216.6 5.8 collective-permute-start.20
  225.0 6.3 %collective-permute-start.22 = (bf16[24,4,128]{2,1,0:T(4,128)(2,1)S(1)}, bf16[24,4,128]{2,1,0:T(4,128)(2,1)S(1)}, u32[]{:S(2)}, u32[]{:S(2)}) collective-permute-start(bf16[24,4,128]{2,1,0:T(4,128)(2,1)S(1)} %get-tuple-element.40), channel_id=1, source_target_pairs={{0,1},{1,2},{2,3},{3,4},{4,5},{5,6},{6,7},{8,9},{9,10},{10,11},{11... | collective-permute-start | bytes 73736 | tf_op jit(solution)/shard_map/ppermute | solution.py:19
  229.8 5.7 collective-permute-start.23
  237.8 5.3 collective-permute-start.24
  248.7 5.7 collective-permute-start.27
  256.7 5.3 collective-permute-start.28
  267.6 5.7 collective-permute-start.31
  292.8 31.6 %all-to-all-start.2 = ((bf16[32,128,128]{2,1,0:T(8,128)(2,1)}), bf16[32,128,128]{2,1,0:T(8,128)(2,1)S(1)}, u32[]{:S(2)}, u32[]{:S(2)}) async-start(bf16[32,128,128]{2,1,0:T(8,128)(2,1)} %select_convert_fusion), calls=%async_computation.2 | async-start | bytes 2097152 | tf_op jit(solution)/shard_map/all_to_all | solution.py:137
  296.8 175.6 %reduce-scatter.5.cloned.1.call-start = ((), (), s32[]{:S(2)}) async-start(), calls=%async_computation.5 | async-start | bytes 1081344 | tf_op jit(solution)/shard_map/reduce_scatter | solution.py:158
  339.5 276.1 %reduce-scatter.7.cloned.1.call-start = ((), (), s32[]{:S(2)}) async-start(), calls=%async_computation.6 | async-start | bytes 4325376
  (28 other events, 203.0 us)
Sparse Core Ops, SparseCore 0:
  339.7 132.6 reduce-scatter.4
  475.3 140.2 reduce-scatter.6
where the time goes:
time: 632 us; the launch traced here: 623 us
  waiting for transfers between devices  364 us (58%)
  starting transfers between devices  100 us (16%)
  other arithmetic  62.1 us (10%)
  local copies, waits for them, and re-layouts  42.8 us (7%)
  matrix products  38.8 us (6%)
  between operations  15.3 us (2%)
    unnamed x3, waiting for transfers between devices  143 us
    reduce_scatter x1, waiting for transfers between devices, local(): lax.psum_scatter(lax.dot_general(piece, dlog, (((0,), (0,)), ((), ())), p...  106 us
    ppermute x16, starting transfers between devices, with_halo(): lax.ppermute(tail, axis, [(i, (i + 1) % count) for i in range(ends)])  61.7 us
    ppermute x16, waiting for transfers between devices, with_halo(): lax.ppermute(head, axis, [((i + 1) % count, i) for i in range(ends)])  55.8 us
    all_to_all x1, waiting for transfers between devices, local(): lax.all_to_all(back_values.reshape(devices, slot_count, species), ('ty',...  27.5 us
    all_to_all x1, waiting for transfers between devices, local(): lax.all_to_all(send_values.reshape(devices, slot_count, species), ('ty',...  27.5 us
    scatter-add x1, other arithmetic, local(): start_field = jnp.zeros((cell_count, species), jnp.float32).at[cell_list]...  23 us
    ppermute x16, starting transfers between devices, with_halo(): lax.ppermute(head, axis, [((i + 1) % count, i) for i in range(ends)])  20.8 us
  transfers between devices with their start and end apart: 37, of which 28 were waited for; matrix products, arithmetic and copies ran while one was open for 7% of the time, Pallas kernels for 0%

commit v1 on v0

v1 whole, which is shorter than its diff:
```python
import functools
import math

import jax
import jax.numpy as jnp
from jax import lax
from jax.experimental import pallas as pl
from jax.experimental.pallas import tpu as pltpu
from jax.sharding import PartitionSpec as P

STEPS = 4
MESH = pl.DeviceIdType.MESH
VMEM_LIMIT = 56 * 1024 * 1024


def bit_list(tiles_y, tiles_x):
    bits = []
    for axis, count in (("ty", tiles_y), ("tx", tiles_x)):
        weight = count // 2
        while weight >= 1:
            bits.append((axis, weight))
            weight //= 2
    return bits


def stream_orders(tiles_y, tiles_x):
    bits = bit_list(tiles_y, tiles_x)
    core = ("ty", 1)
    rows = [b for b in bits if b[0] == "ty" and b[1] > 1]
    near = [b for b in bits if b[0] == "tx" and b[1] < tiles_x // 4]
    far = [b for b in bits if b[0] == "tx" and b[1] >= tiles_x // 4][::-1]
    return (
        [core] + rows + near + far,
        [core] + near + far + rows,
        [core] + far + near + rows,
    )


def stream_shapes(bits, order, rows, cols):
    left = list(bits)
    held, got = [], []
    for bit in order:
        place = left.index(bit)
        before, after = 2**place, 2 ** (len(left) - place - 1)
        held.append((before, 2, after, rows, cols))
        got.append((before, after, rows, cols))
        left.remove(bit)
    return held, got


def sum_kernel(tiles_y, tiles_x, plan, *refs):
    streams = len(plan)
    stages = len(plan[0][0])
    gin, gout, out_in, out_out = refs[:4]
    rest = list(refs[4:])
    got = [[rest.pop(0) for _ in range(stages)] for _ in range(streams)]
    held = [[None] + [rest.pop(0) for _ in range(stages - 1)] for _ in range(streams)]
    send_sem, recv_sem = rest
    at = {"ty": lax.axis_index("ty"), "tx": lax.axis_index("tx")}

    def side(bit):
        return lax.rem(at[bit[0]] // bit[1], 2)

    def partner(bit):
        axis, weight = bit
        moved = at[axis] + weight * (1 - 2 * side(bit))
        return (moved, at["tx"]) if axis == "ty" else (at["ty"], moved)

    barrier = pltpu.get_barrier_semaphore()
    for bit in bit_list(tiles_y, tiles_x):
        pl.semaphore_signal(barrier, inc=1, device_id=partner(bit), device_id_type=MESH)
    pl.semaphore_wait(barrier, stages)

    def source(s, k, which):
        order, first, cols = plan[s][0], plan[s][1], plan[s][2]
        if k > 0:
            return held[s][k].at[:, which]
        if first is None:
            return gout.at[:, which]
        return gin.at[:, which, :, :, first : first + cols]

    def copy(s, k):
        bit = plan[s][0][k]
        return pltpu.make_async_remote_copy(
            src_ref=source(s, k, 1 - side(bit)),
            dst_ref=got[s][k],
            send_sem=send_sem.at[s, k],
            recv_sem=recv_sem.at[s, k],
            device_id=partner(bit),
            device_id_type=MESH,
        )

    for s in range(streams):
        copy(s, 0).start()
    for k in range(stages):
        for s in range(streams):
            copy(s, k).wait_recv()
            mine = source(s, k, side(plan[s][0][k]))
            before, after = got[s][k].shape[:2]
            if k + 1 < stages:
                nxt = held[s][k + 1]
                after_n = nxt.shape[2]

                def add(i, _, mine=mine, theirs=got[s][k], nxt=nxt, after=after, after_n=after_n):
                    a, b = i // after, lax.rem(i, after)
                    nxt[i // (2 * after_n), lax.rem(i // after_n, 2), lax.rem(i, after_n)] = (
                        mine[a, b] + theirs[a, b]
                    )
                    return 0

                lax.fori_loop(0, before * after, add, 0)
                copy(s, k + 1).start()
            else:
                total = mine[0, 0] + got[s][k][0, 0]
                first, cols = plan[s][1], plan[s][2]
                if first is None:
                    out_out[...] = total
                else:
                    out_in[:, first : first + cols] = total
    for k in range(stages):
        for s in range(streams):
            copy(s, k).wait_send()


def sum_grads(grad_in, grad_out, tiles_y, tiles_x):
    devices = tiles_y * tiles_x
    rows_in, cols_in = grad_in.shape[0] // devices, grad_in.shape[1]
    rows_out, cols_out = grad_out.shape[0] // devices, grad_out.shape[1]
    bits = bit_list(tiles_y, tiles_x)
    orders = stream_orders(tiles_y, tiles_x)
    tile = cols_in // 16
    plan = [
        (orders[0], 0, 7 * tile, rows_in),
        (orders[1], 7 * tile, 7 * tile, rows_in),
        (orders[2], 14 * tile, 2 * tile, rows_in),
        (orders[2], None, cols_out, rows_out),
    ]
    held_all, got_all = [], []
    for order, first, cols, rows in plan:
        held, got = stream_shapes(bits, order, rows, cols)
        held_all += [pltpu.VMEM(s, jnp.float32) for s in held[1:]]
        got_all += [pltpu.VMEM(s, jnp.float32) for s in got]
    core_before, core_after = tiles_y // 2, tiles_x
    stages = len(bits)
    return pl.pallas_call(
        functools.partial(sum_kernel, tiles_y, tiles_x, plan),
        out_shape=(
            jax.ShapeDtypeStruct((rows_in, cols_in), jnp.float32),
            jax.ShapeDtypeStruct((rows_out, cols_out), jnp.float32),
        ),
        in_specs=[pl.BlockSpec(memory_space=pltpu.VMEM)] * 2,
        out_specs=(pl.BlockSpec(memory_space=pltpu.VMEM),) * 2,
        scratch_shapes=got_all
        + held_all
        + [
            pltpu.SemaphoreType.DMA((len(plan), stages)),
            pltpu.SemaphoreType.DMA((len(plan), stages)),
        ],
        compiler_params=pltpu.CompilerParams(
            collective_id=1, has_side_effects=True, vmem_limit_bytes=VMEM_LIMIT
        ),
        name="sum_grads",
    )(
        grad_in.reshape(core_before, 2, core_after, rows_in, cols_in),
        grad_out.reshape(core_before, 2, core_after, rows_out, cols_out),
    )


DIRS = ((-1, 0), (1, 0), (0, -1), (0, 1), (-1, -1), (-1, 1), (1, -1), (1, 1))


def raster_kernel(
    tiles_y,
    tiles_x,
    start_ref,
    taps_y_ref,
    taps_x_ref,
    rate_ref,
    cap_ref,
    obs_ref,
    sur_ref,
    density_ref,
    g0_ref,
    field,
    part,
    mids,
    y_out,
    y_in,
    send_sem,
    recv_sem,
):
    height, width, species = start_ref.shape
    at_y, at_x = lax.axis_index("ty"), lax.axis_index("tx")
    blocks = width // 8

    def exists(d):
        dy, dx = DIRS[d]
        conds = []
        if dy == -1:
            conds.append(at_y > 0)
        if dy == 1:
            conds.append(at_y < tiles_y - 1)
        if dx == -1:
            conds.append(at_x > 0)
        if dx == 1:
            conds.append(at_x < tiles_x - 1)
        return conds[0] if len(conds) == 1 else jnp.logical_and(*conds)

    def device(d):
        return (at_y + DIRS[d][0], at_x + DIRS[d][1])

    zero_rows = jnp.zeros((4, width + 16, species), jnp.float32)
    zero_cols = jnp.zeros((height, 8, species), jnp.float32)
    for p in range(2):
        field[p, 0:4] = zero_rows
        field[p, height + 4 : height + 8] = zero_rows
        field[p, 4 : height + 4, 0:8] = zero_cols
        field[p, 4 : height + 4, width + 8 : width + 16] = zero_cols
        for s in range(2):
            y_in[p, s] = jnp.zeros((4, width, species), jnp.bfloat16)

    def load_row(i, _):
        field[0, i + 4, 8 : width + 8] = start_ref[i]
        return 0

    lax.fori_loop(0, height, load_row, 0)

    barrier = pltpu.get_barrier_semaphore()
    for d in range(8):

        @pl.when(exists(d))
        def _(d=d):
            pl.semaphore_signal(barrier, inc=1, device_id=device(d), device_id_type=MESH)

    count_y = jnp.where(at_y > 0, 2, 1) + jnp.where(at_y < tiles_y - 1, 1, 0)
    count_x = jnp.where(at_x > 0, 2, 1) + jnp.where(at_x < tiles_x - 1, 1, 0)
    pl.semaphore_wait(barrier, count_y * count_x - 1)

    rows_of = {-1: (4, 8), 0: (4, height + 4), 1: (height, height + 4)}
    cols_of = {-1: (8, 16), 0: (8, width + 8), 1: (width, width + 8)}
    rows_to = {-1: (height + 4, height + 8), 0: (4, height + 4), 1: (0, 4)}
    cols_to = {-1: (width + 8, width + 16), 0: (8, width + 8), 1: (0, 8)}

    def copy(t, d):
        dy, dx = DIRS[d]
        p = t % 2
        if dx == 0:
            src, dst = y_out.at[p, 0 if dy == -1 else 1], y_in.at[p, 1 if dy == -1 else 0]
        else:
            r0, r1 = rows_of[dy]
            c0, c1 = cols_of[dx]
            src = field.at[p, r0:r1, c0:c1]
            r0, r1 = rows_to[dy]
            c0, c1 = cols_to[dx]
            dst = field.at[p, r0:r1, c0:c1]
        return pltpu.make_async_remote_copy(
            src_ref=src,
            dst_ref=dst,
            send_sem=send_sem.at[t, d],
            recv_sem=recv_sem.at[t, d],
            device_id=device(d),
            device_id_type=MESH,
        )

    def start(t, dirs):
        for d in dirs:

            @pl.when(exists(d))
            def _(d=d):
                copy(t, d).start()

    def stage_rows(t):
        p = t % 2
        for s, r0 in ((0, 4), (1, height)):
            for r in range(4):
                y_out[p, s, r] = field[p, r0 + r, 8 : width + 8].astype(jnp.bfloat16)

    opposite = [DIRS.index((-dy, -dx)) for dy, dx in DIRS]

    def finish(t):
        p = t % 2
        for d in range(8):

            @pl.when(exists(d))
            def _(d=d):
                copy(t, opposite[d]).wait_recv()

        for s, r0 in ((0, 0), (1, height + 4)):
            for r in range(4):
                field[p, r0 + r, 8 : width + 8] = y_in[p, s, r].astype(jnp.float32)

    def sent(t):
        for d in range(8):

            @pl.when(exists(d))
            def _(d=d):
                copy(t, d).wait_send()

    rate = jnp.broadcast_to(rate_ref[...], (8, species))
    grow = 1.0 + rate
    slope = rate / jnp.broadcast_to(cap_ref[...], (8, species))

    stage_rows(0)
    start(0, range(8))

    for t in range(2 * STEPS):
        p = t % 2
        order = range(9) if t < STEPS else range(8, -1, -1)
        taps_y = [taps_y_ref[a] for a in order]
        taps_x = [taps_x_ref[a] for a in order]
        finish(t)

        def down(c, _, p=p, taps_y=taps_y):
            cols = pl.ds(pl.multiple_of(c * 8, 8), 8)
            rows = [field[p, i, cols, :] for i in range(height + 8)]
            for i in range(height):
                pairs = [taps_y[a] * rows[i + a] for a in range(9)]
                while len(pairs) > 1:
                    pairs = [sum(pairs[j : j + 2][1:], pairs[j]) for j in range(0, len(pairs), 2)]
                part[i, cols, :] = pairs[0]
            return 0

        lax.fori_loop(0, blocks + 2, down, 0)
        if t + 1 < 2 * STEPS and t >= 1:
            sent(t - 1)

        def across(i, t=t, p=p, taps_x=taps_x):
            if t == STEPS - 1:
                seen = jnp.broadcast_to(sur_ref[pl.ds(i, 1), :], (width, width)).T
            for c in range(blocks):
                cols = slice(8 * c, 8 * c + 8)
                pairs = [taps_x[b] * part[i, 8 * c + 4 + b : 8 * c + 12 + b, :] for b in range(9)]
                while len(pairs) > 1:
                    pairs = [sum(pairs[j : j + 2][1:], pairs[j]) for j in range(0, len(pairs), 2)]
                value = pairs[0]
                if t == 2 * STEPS - 1:
                    g0_ref[i, cols, :] = value
                    continue
                if t < STEPS:
                    inverse = 1.0 / (1.0 + slope * value)
                    if t < STEPS - 1:
                        mids[t, i, cols, :] = value
                    new = value * grow * inverse
                    if t == STEPS - 1:
                        density_ref[i, cols, :] = new
                        ratio = obs_ref[i, cols, :].astype(jnp.float32) / new
                        value = seen[cols, :] * (1.0 - ratio)
                        new = value * grow * inverse * inverse
                else:
                    mid = mids[2 * STEPS - 2 - t, i, cols, :]
                    inverse = 1.0 / (1.0 + slope * mid)
                    new = value * grow * inverse * inverse
                field[1 - p, i + 4, 8 + 8 * c : 16 + 8 * c, :] = new

        def border(k, _):
            across(jnp.where(k < 4, k, k + (height - 8)))
            return 0

        def middle(k, _):
            across(k + 4)
            return 0

        lax.fori_loop(0, 8, border, 0)
        if t + 1 < 2 * STEPS:
            stage_rows(t + 1)
            start(t + 1, (0, 1, 4, 5, 6, 7))
        lax.fori_loop(0, height - 8, middle, 0)
        if t + 1 < 2 * STEPS:
            start(t + 1, (2, 3))
    sent(2 * STEPS - 2)
    sent(2 * STEPS - 1)


def raster_steps(start, taps_y, taps_x, rate, capacity, observed, seen, tiles_y, tiles_x):
    height, width, species = start.shape

    def wide(taps):
        return jnp.broadcast_to(taps.T[:, None, :], (9, 8, species))

    vmem = pl.BlockSpec(memory_space=pltpu.VMEM)
    return pl.pallas_call(
        functools.partial(raster_kernel, tiles_y, tiles_x),
        out_shape=(jax.ShapeDtypeStruct(start.shape, jnp.float32),) * 2,
        in_specs=[vmem] * 7,
        out_specs=(vmem,) * 2,
        scratch_shapes=[
            pltpu.VMEM((2, height + 8, width + 16, species), jnp.float32),
            pltpu.VMEM((height, width + 16, species), jnp.float32),
            pltpu.VMEM((STEPS - 1, height, width, species), jnp.float32),
            pltpu.VMEM((2, 2, 4, width, species), jnp.bfloat16),
            pltpu.VMEM((2, 2, 4, width, species), jnp.bfloat16),
            pltpu.SemaphoreType.DMA((2 * STEPS, 8)),
            pltpu.SemaphoreType.DMA((2 * STEPS, 8)),
        ],
        compiler_params=pltpu.CompilerParams(
            collective_id=2, has_side_effects=True, vmem_limit_bytes=VMEM_LIMIT
        ),
        name="raster_steps",
    )(
        start,
        wide(taps_y),
        wide(taps_x),
        rate.reshape(1, species),
        capacity.reshape(1, species),
        observed,
        seen,
    )


def normalize(taps):
    return taps / jnp.sum(taps, axis=1, keepdims=True)


def silu_slope(value):
    sigmoid_v = jax.nn.sigmoid(value)
    return sigmoid_v + value * sigmoid_v * (1.0 - sigmoid_v)


def local(
    covariates,
    w_in,
    b_in,
    w_out,
    b_out,
    owner,
    land_cell,
    row_taps,
    col_taps,
    rate,
    capacity,
    observed,
    surveyed,
):
    row_count = covariates.shape[0]
    tiles_y = lax.axis_size("ty")
    tiles_x = lax.axis_size("tx")
    devices = tiles_y * tiles_x
    slot_count = 2 * row_count // devices
    height, tile_width, species = observed.shape
    cell_count = height * tile_width
    preact = jnp.dot(covariates, w_in, preferred_element_type=jnp.float32) + b_in
    hidden = jax.nn.silu(preact).astype(jnp.bfloat16)
    log_rate = jnp.dot(hidden, w_out, preferred_element_type=jnp.float32) + b_out
    intensity = jnp.exp(log_rate)
    sent = intensity.astype(jnp.bfloat16)
    owner_rows = owner[:, 0]
    onehot = (owner_rows[:, None] == jnp.arange(devices, dtype=jnp.int32)[None, :]).astype(
        jnp.int32
    )
    before = jnp.cumsum(onehot, axis=0) - onehot
    slot_idx = jnp.sum(before * onehot, axis=1)
    flat_slot = owner_rows * slot_count + slot_idx
    send_values = jnp.zeros((devices * slot_count, species), jnp.bfloat16).at[flat_slot].set(sent)
    send_cells = (
        jnp.full((devices * slot_count,), cell_count, jnp.int32).at[flat_slot].set(land_cell)
    )
    got_values, got_cells = (
        lax.all_to_all(
            send_values.reshape(devices, slot_count, species),
            ("ty", "tx"),
            split_axis=0,
            concat_axis=0,
            tiled=True,
        ),
        lax.all_to_all(
            send_cells.reshape(devices, slot_count),
            ("ty", "tx"),
            split_axis=0,
            concat_axis=0,
            tiled=True,
        ),
    )
    cell_list = got_cells.reshape(-1)
    start_field = (
        jnp.zeros((cell_count, species), jnp.float32)
        .at[cell_list]
        .add(got_values.reshape(-1, species).astype(jnp.float32), mode="drop")
    )
    field = 0.1 + start_field.reshape(height, tile_width, species)
    taps_y = normalize(row_taps)
    taps_x = normalize(col_taps)
    scale = 1.0 / math.sqrt(row_count * devices)
    seen = surveyed.astype(jnp.float32) * scale
    field, grad_field = raster_steps(
        field, taps_y, taps_x, rate, capacity, observed, seen, tiles_y, tiles_x
    )
    back_values = jnp.take(
        grad_field.reshape(cell_count, species), cell_list, axis=0, mode="fill", fill_value=0.0
    ).astype(jnp.bfloat16)
    home_values = lax.all_to_all(
        back_values.reshape(devices, slot_count, species),
        ("ty", "tx"),
        split_axis=0,
        concat_axis=0,
        tiled=True,
    )
    returned = home_values.reshape(devices * slot_count, species)[flat_slot]
    dlog = (returned.astype(jnp.float32) * intensity).astype(jnp.bfloat16)
    dhidden = lax.dot_general(
        dlog, w_out, (((1,), (1,)), ((), ())), preferred_element_type=jnp.float32
    )
    dpre = (dhidden * silu_slope(preact)).astype(jnp.bfloat16)
    grad_w_in, grad_w_out = sum_grads(
        lax.dot_general(
            covariates, dpre, (((0,), (0,)), ((), ())), preferred_element_type=jnp.float32
        ),
        lax.dot_general(
            hidden, dlog, (((0,), (0,)), ((), ())), preferred_element_type=jnp.float32
        ),
        tiles_y,
        tiles_x,
    )
    return (field, grad_w_in, grad_w_out)


def solution(mesh):
    in_specs = (
        P(("ty", "tx"), None),
        P(),
        P(),
        P(),
        P(),
        P(("ty", "tx"), None),
        P(("ty", "tx")),
        P(),
        P(),
        P(),
        P(),
        P("ty", "tx", None),
        P("ty", "tx"),
    )
    out_specs = (P("ty", "tx", None), P(("ty", "tx"), None), P(("ty", "tx"), None))
    return jax.shard_map(local, mesh=mesh, in_specs=in_specs, out_specs=out_specs, check_vma=False)
```

time: 632 us -> 295 us (0.47); the launches traced: 623 us -> 294 us
  waiting for transfers between devices: 364 us -> 54.4 us
  Pallas kernels: 0 us -> 96.9 us
  starting transfers between devices: 100 us -> 18.8 us
  other arithmetic: 62.1 us -> 45.6 us
  between operations: 15.3 us -> 0.85 us
    unnamed x3 -> x0, waiting for transfers between devices: 143 us -> none
    reduce_scatter x1 -> x0, waiting for transfers between devices: 106 us -> none  [local(): lax.psum_scatter(lax.dot_general(piece, dlog, (((0,), (0,)), ((), ())), p...]
    pallas_call x0 -> x2, Pallas kernels: none -> 96.9 us  [the longest x1 56 us: raster_steps(): pl.pallas_call(functools.partial(raster_kernel, tiles_y, tiles_x), out_sh...]
    ppermute x32 -> x0, starting transfers between devices: 82.5 us -> none  [the longest x16 61.7 us: with_halo(): lax.ppermute(tail, axis, [(i, (i + 1) % count) for i in range(ends)])]
    ppermute x32 -> x0, waiting for transfers between devices: 59.2 us -> none  [the longest x16 55.8 us: with_halo(): lax.ppermute(head, axis, [((i + 1) % count, i) for i in range(ends)])]
    convert_element_type x9 -> x0, other arithmetic: 7.48 us -> none  [the longest x4 6.4 us: local(): grad_mid.astype(jnp.bfloat16)]
    dot_general x2 -> x3, matrix products: 25.6 us -> 23.4 us  [the longest x1 9.95 us: local(): lax.dot_general(dlog, w_out, (((1,), (1,)), ((), ())), preferred_element_...]
  transfers between devices with their start and end apart: 37 -> 3, of which waited for: 28 -> 2; matrix products, arithmetic and copies ran while one was open for 7% -> 7% of each run, Pallas kernels for 0% -> 0%
where the time goes in v1:
time: 295 us; the launch traced here: 294 us
  Pallas kernels  96.9 us (33%)
  waiting for transfers between devices  54.4 us (18%)
  other arithmetic  45.6 us (15%)
  local copies, waits for them, and re-layouts  41.2 us (14%)
  matrix products  36.5 us (12%)
  starting transfers between devices  18.8 us (6%)
    pallas_call x1, Pallas kernels, raster_steps(): pl.pallas_call(functools.partial(raster_kernel, tiles_y, tiles_x), out_sh...  56 us
    pallas_call x1, Pallas kernels, sum_grads(): pl.pallas_call(functools.partial(sum_kernel, tiles_y, tiles_x, plan), out...  41 us
    all_to_all x1, waiting for transfers between devices, local(): lax.all_to_all(back_values.reshape(devices, slot_count, species), ('ty',...  27.6 us
    all_to_all x1, waiting for transfers between devices, local(): lax.all_to_all(send_values.reshape(devices, slot_count, species), ('ty',...  26.8 us
    scatter-add x1, other arithmetic, local(): start_field = jnp.zeros((cell_count, species), jnp.float32).at[cell_list]...  23.7 us
    gather x1, local copies, waits for them, and re-layouts, local(): jnp.take(grad_field.reshape(cell_count, species), cell_list, axis=0, mode...  15.6 us
    dot_general x1, matrix products, local(): jnp.dot(covariates, w_in, preferred_element_type=jnp.float32) + b_in  10.7 us
    dot_general x1, matrix products, local(): lax.dot_general(dlog, w_out, (((1,), (1,)), ((), ())), preferred_element_...  9.95 us
  transfers between devices with their start and end apart: 3, of which 2 were waited for; matrix products, arithmetic and copies ran while one was open for 7% of the time, Pallas kernels for 0%

profile of v1, /device:TPU:0, one launch (start us, length us, event | category | flops | bytes accessed | tf_op | source)
XLA Modules:
  0.0 294.2 jit_solution(9042857742205502472)
XLA Ops:
  0.6 0.9 fusion.11
  1.5 9.1 %reduce-window.6 = s32[32,16,128]{2,1,0:T(8,128)S(1)} reduce-window(s32[32,16,128]{2,1,0:T(8,128)S(1)} %fusion.11, s32[]{:T(128)} %constant.14.clone.1), window={size=1x1x128 pad=0_0x0_0x127_0}, to_apply=%region_0.1 | reduce-window | flops 8323072 | bytes 524292 | tf_op jit(solution)/shard_map/reduce-window
  12.9 8.8 %scatter_custom_fusion = s32[4096]{0:T(1024)} fusion(s32[2048]{0:T(1024)S(1)} %bitcast.70, s32[2048]{0:T(1024)} %param.19, s32[]{:T(128)} %constant.11.clone.1), kind=kCustom, calls=%fused_computation.35 | custom fusion | bytes 16896 | tf_op jit(solution)/shard_map/scatter | solution.py:455
  21.6 7.3 %all-to-all-start = ((s32[32,1,128]{2,1,0:T(1,128)}), s32[32,1,128]{2,1,0:T(1,128)S(1)}, u32[]{:S(2)}, u32[]{:S(2)}) async-start(s32[32,1,128]{2,1,0:T(1,128)} %bitcast.7), calls=%async_computation | async-start | bytes 32768 | tf_op jit(solution)/shard_map/all_to_all | solution.py:465
  29.0 10.7 %fusion = (bf16[2048,2048]{1,0:T(8,128)(2,1)S(1)}, f32[2048,2048]{1,0:T(8,128)}) fusion(f32[2048]{0:T(1024)} %param.15, bf16[2048,512]{1,0:T(8,128)(2,1)S(1)} %copy-done, bf16[512,2048]{1,0:T(8,128)(2,1)} %param.14), kind=kOutput, calls=%fused_computation.8 | convolution fusion | flops 4320133120 | bytes 29368320 | tf_op jit(solution)/shard_map/dot_general | solution.py:441
  39.7 3.2 %copy-done.1 = bf16[2048,2048]{1,0:T(8,128)(2,1)} copy-done((bf16[2048,2048]{1,0:T(8,128)(2,1)}, bf16[2048,2048]{1,0:T(8,128)(2,1)S(1)}, u32[]{:S(2)}) %copy-start.1) | copy-done | bytes 8388632
  43.0 2.4 fusion.1
  45.3 6.8 %scatter_custom_fusion.1 = bf16[4096,128]{1,0:T(8,128)(2,1)} fusion(s32[2048]{0:T(1024)S(1)} %bitcast.71, f32[2048,128]{1,0:T(8,128)S(1)} %fusion.1, bf16[]{:T(256)} %constant.17.clone.1), kind=kCustom, calls=%fused_computation.15 | custom fusion | flops 262144 | bytes 2097154 | tf_op jit(solution)/shard_map/scatter | solution.py:453
  52.1 6.0 %all-to-all-start.1 = ((bf16[32,128,128]{2,1,0:T(8,128)(2,1)}), bf16[32,128,128]{2,1,0:T(8,128)(2,1)}, u32[]{:S(2)}, u32[]{:S(2)}) async-start(bf16[32,128,128]{2,1,0:T(8,128)(2,1)} %bitcast.59), calls=%async_computation.1 | async-start | bytes 2097152 | tf_op jit(solution)/shard_map/all_to_all | solution.py:458
  58.8 26.8 %all-to-all-done.1 = bf16[32,128,128]{2,1,0:T(8,128)(2,1)} async-done(((bf16[32,128,128]{2,1,0:T(8,128)(2,1)}), bf16[32,128,128]{2,1,0:T(8,128)(2,1)}, u32[]{:S(2)}, u32[]{:S(2)}) %all-to-all-start.1) | async-done | bytes 1048608 | tf_op jit(solution)/shard_map/all_to_all | solution.py:458
  85.6 23.7 %scatter_custom_fusion.2 = f32[2048,128]{1,0:T(8,128)} fusion(s32[4096]{0:T(1024)S(1)} %bitcast.68, bf16[4096,128]{1,0:T(8,128)(2,1)} %bitcast.24, f32[]{:T(128)} %constant.10.clone.1), kind=kCustom, calls=%fused_computation.11 | custom fusion | flops 1048576 | bytes 2097156 | tf_op jit(solution)/shard_map/scatter-add | solution.py:477
  110.6 56.0 %raster_steps.1 = (f32[16,128,128]{2,1,0:T(8,128)}, f32[16,128,128]{2,1,0:T(8,128)}) custom-call(f32[16,128,128]{2,1,0:T(8,128)} %bitcast.60, f32[9,8,128]{2,1,0:T(8,128)} %broadcast_in_dim.17.taps_y_ref, f32[9,8,128]{2,1,0:T(8,128)} %broadcast_in_dim.18.taps_x_ref, f32[1,128]{1,0:T(1,128)} %bitcast.73, f32[1,128]{1,0:T(1,128)} %bitcast.74, ...), custom_call_target="tpu_custom_call" | custom-call | tf_op jit(solution)/shard_map/raster_steps/pallas_call | solution.py:381
  166.6 15.6 %gather_fusion = bf16[4096,128]{1,0:T(8,128)(2,1)} fusion(f32[2048,128]{1,0:T(8,128)} %bitcast.54, s32[4096]{0:T(1024)S(1)} %broadcast_clamp_fusion), kind=kCustom, calls=%fused_computation | custom fusion | bytes 2113536 | tf_op jit(solution)/shard_map/jit(_take)/gather | solution.py:487
  182.2 2.5 select_convert_fusion
  184.7 5.5 %all-to-all-start.2 = ((bf16[32,128,128]{2,1,0:T(8,128)(2,1)}), bf16[32,128,128]{2,1,0:T(8,128)(2,1)S(1)}, u32[]{:S(2)}, u32[]{:S(2)}) async-start(bf16[32,128,128]{2,1,0:T(8,128)(2,1)} %select_convert_fusion), calls=%async_computation.2 | async-start | bytes 2097152 | tf_op jit(solution)/shard_map/all_to_all | solution.py:490
  190.3 27.6 %all-to-all-done.2 = bf16[32,128,128]{2,1,0:T(8,128)(2,1)S(1)} async-done(((bf16[32,128,128]{2,1,0:T(8,128)(2,1)}), bf16[32,128,128]{2,1,0:T(8,128)(2,1)S(1)}, u32[]{:S(2)}, u32[]{:S(2)}) %all-to-all-start.2) | async-done | bytes 1048608 | tf_op jit(solution)/shard_map/all_to_all | solution.py:490
  217.9 8.0 %gather_fusion.1 = bf16[2048,128]{1,0:T(8,128)(2,1)} fusion(bf16[4096,128]{1,0:T(8,128)(2,1)S(1)} %bitcast.55, s32[2048]{0:T(1024)S(1)} %broadcast_clamp_fusion.1), kind=kCustom, calls=%fused_computation.1 | custom fusion | bytes 1056768 | tf_op jit(solution)/shard_map/gather | solution.py:497
  225.9 7.2 %fusion.14 = f32[2048,128]{1,0:T(8,128)} fusion(bf16[2048,2048]{1,0:T(8,128)(2,1)} %copy-done.1, f32[2048,128]{1,0:T(8,128)} %copy-done.2, bf16[2048,128]{1,0:T(8,128)(2,1)} %gather_fusion.1), kind=kOutput, calls=%fused_computation.38 | convolution fusion | flops 1074528256 | bytes 11010048 | tf_op jit(solution)/shard_map/dot_general | solution.py:507
  233.2 9.9 %multiply_convert_fusion = bf16[2048,2048]{1,0:T(8,128)(2,1)S(1)} fusion(f32[2048,2048]{1,0:T(8,128)} %get-tuple-element.12, bf16[2048,128]{1,0:T(8,128)(2,1)S(1)} %copy-done.10, f32[2048]{0:T(1024)S(1)} %copy-done.11, f32[2048,128]{1,0:T(8,128)S(1)} %copy-done.3, bf16[2048,128]{1,0:T(8,128)(2,1)S(1)} %copy-done.4), kind=kOutput, calls=%fused_computation.5 | convolution fusion | flops 1116471296 | bytes 27271168 | tf_op jit(solution)/shard_map/dot_general | solution.py:499
  243.1 6.2 %fusion.15 = f32[2048,512]{0,1:T(8,128)} fusion(bf16[2048,2048]{1,0:T(8,128)(2,1)S(1)} %multiply_convert_fusion, bf16[2048,512]{1,0:T(8,128)(2,1)S(1)} %copy-done), kind=kOutput, calls=%fused_computation.39 | convolution fusion | flops 4294967296 | bytes 14680064 | tf_op jit(solution)/shard_map/dot_general | solution.py:504
  249.3 41.0 %sum_grads.1 = (f32[16,2048]{1,0:T(8,128)}, f32[64,128]{1,0:T(8,128)}) custom-call(f32[2,2,8,16,2048]{4,3,2,1,0:T(8,128)} %bitcast.57, f32[2,2,8,64,128]{4,3,2,1,0:T(8,128)} %bitcast.56), custom_call_target="tpu_custom_call" | custom-call | tf_op jit(solution)/shard_map/sum_grads/pallas_call | solution.py:145
  290.3 1.0 copy.26
  291.3 1.6 copy.27
  292.8 1.4 copy.28
  (43 shorter events, 4.2 us)
Async XLA Ops:
  0.6 28.3 %copy-start = (bf16[2048,512]{1,0:T(8,128)(2,1)S(1)}, bf16[2048,512]{1,0:T(8,128)(2,1)}, u32[]{:S(2)}) copy-start(bf16[2048,512]{1,0:T(8,128)(2,1)} %param.13) | copy-start | bytes 6291460
  21.6 30.5 %all-to-all-start = ((s32[32,1,128]{2,1,0:T(1,128)}), s32[32,1,128]{2,1,0:T(1,128)S(1)}, u32[]{:S(2)}, u32[]{:S(2)}) async-start(s32[32,1,128]{2,1,0:T(1,128)} %bitcast.7), calls=%async_computation | async-start | bytes 32768 | tf_op jit(solution)/shard_map/all_to_all | solution.py:465
  29.0 14.0 %copy-start.9 = (bf16[2048,128]{1,0:T(8,128)(2,1)S(1)}, bf16[2048,128]{1,0:T(8,128)(2,1)}, u32[]{:S(2)}) copy-start(bf16[2048,128]{1,0:T(8,128)(2,1)} %param.16) | copy-start | bytes 1572868
  29.0 14.0 %copy-start.12 = (f32[128]{0:T(128)S(1)}, f32[128]{0:T(128)}, u32[]{:S(2)}) copy-start(f32[128]{0:T(128)} %param.17) | copy-start | bytes 1540
  39.7 3.2 %copy-start.1 = (bf16[2048,2048]{1,0:T(8,128)(2,1)}, bf16[2048,2048]{1,0:T(8,128)(2,1)S(1)}, u32[]{:S(2)}) copy-start(bf16[2048,2048]{1,0:T(8,128)(2,1)S(1)} %get-tuple-element.11) | copy-start | bytes 25165828
  39.7 18.3 %copy-start.6 = (f32[128,9]{0,1:T(8,128)S(1)}, f32[128,9]{0,1:T(8,128)}, u32[]{:S(2)}) copy-start(f32[128,9]{0,1:T(8,128)} %param.20) | copy-start | bytes 13828
  39.7 18.4 %copy-start.7 = (f32[128,9]{0,1:T(8,128)S(1)}, f32[128,9]{0,1:T(8,128)}, u32[]{:S(2)}) copy-start(f32[128,9]{0,1:T(8,128)} %param.21) | copy-start | bytes 13828
  39.7 18.4 %copy-start.8 = (s32[16,128]{1,0:T(8,128)S(1)}, s32[16,128]{1,0:T(8,128)}, u32[]{:S(2)}) copy-start(s32[16,128]{1,0:T(8,128)} %param.25) | copy-start | bytes 24580
  45.3 136.9 %copy-start.2 = (f32[2048,128]{1,0:T(8,128)}, f32[2048,128]{1,0:T(8,128)S(1)}, u32[]{:S(2)}) copy-start(f32[2048,128]{1,0:T(8,128)S(1)} %fusion.1) | copy-start | bytes 3145732
  52.1 33.5 %all-to-all-start.1 = ((bf16[32,128,128]{2,1,0:T(8,128)(2,1)}), bf16[32,128,128]{2,1,0:T(8,128)(2,1)}, u32[]{:S(2)}, u32[]{:S(2)}) async-start(bf16[32,128,128]{2,1,0:T(8,128)(2,1)} %bitcast.59), calls=%async_computation.1 | async-start | bytes 2097152 | tf_op jit(solution)/shard_map/all_to_all | solution.py:458
  184.7 33.1 %all-to-all-start.2 = ((bf16[32,128,128]{2,1,0:T(8,128)(2,1)}), bf16[32,128,128]{2,1,0:T(8,128)(2,1)S(1)}, u32[]{:S(2)}, u32[]{:S(2)}) async-start(bf16[32,128,128]{2,1,0:T(8,128)(2,1)} %select_convert_fusion), calls=%async_computation.2 | async-start | bytes 2097152 | tf_op jit(solution)/shard_map/all_to_all | solution.py:490
  217.9 15.3 %copy-start.11 = (f32[2048]{0:T(1024)S(1)}, f32[2048]{0:T(1024)}, u32[]{:S(2)}) copy-start(f32[2048]{0:T(1024)} %param.15) | copy-start | bytes 24580
  225.9 7.3 %copy-start.3 = (f32[2048,128]{1,0:T(8,128)S(1)}, f32[2048,128]{1,0:T(8,128)}, u32[]{:S(2)}) copy-start(f32[2048,128]{1,0:T(8,128)} %copy-done.2) | copy-start | bytes 3145732
  225.9 7.3 %copy-start.4 = (bf16[2048,128]{1,0:T(8,128)(2,1)S(1)}, bf16[2048,128]{1,0:T(8,128)(2,1)}, u32[]{:S(2)}) copy-start(bf16[2048,128]{1,0:T(8,128)(2,1)} %gather_fusion.1) | copy-start | bytes 1572868
  225.9 7.3 %copy-start.10 = (bf16[2048,128]{1,0:T(8,128)(2,1)S(1)}, bf16[2048,128]{1,0:T(8,128)(2,1)}, u32[]{:S(2)}) copy-start(bf16[2048,128]{1,0:T(8,128)(2,1)} %param.16) | copy-start | bytes 1572868
  243.1 47.2 %copy-start.5 = (f32[16,128,128]{2,1,0:T(8,128)S(1)}, f32[16,128,128]{2,1,0:T(8,128)}, u32[]{:S(2)}) copy-start(f32[16,128,128]{2,1,0:T(8,128)} %get-tuple-element.16) | copy-start | bytes 3145732

commit v2 on v1

--- a/solution.py
+++ b/solution.py
@@ -407,13 +407,307 @@
     )
 
 
+def local_call(body, shapes, args, scratch=(), name=None, **extra):
+    vmem = pl.BlockSpec(memory_space=pltpu.VMEM)
+    many = isinstance(shapes, tuple)
+    return pl.pallas_call(
+        body,
+        out_shape=shapes,
+        in_specs=[vmem] * len(args),
+        out_specs=(vmem,) * len(shapes) if many else vmem,
+        scratch_shapes=list(scratch),
+        compiler_params=pltpu.CompilerParams(vmem_limit_bytes=VMEM_LIMIT),
+        name=name,
+        **extra,
+    )(*args)
+
+
+def sigmoid(value):
+    return 0.5 + 0.5 * jnp.tanh(0.5 * value)
+
+
+def forward_kernel(x_ref, w_in_ref, b_in_ref, w_out_ref, b_out_ref, intensity_ref):
+    x = x_ref[...]
+    hidden_units = w_in_ref.shape[1]
+    log_rate = b_out_ref[...]
+    for c in range(0, hidden_units, 512):
+        pre = jnp.dot(x, w_in_ref[:, c : c + 512], preferred_element_type=jnp.float32)
+        pre = pre + b_in_ref[:, c : c + 512]
+        hidden = (pre * sigmoid(pre)).astype(jnp.bfloat16)
+        log_rate = log_rate + jnp.dot(
+            hidden, w_out_ref[c : c + 512, :], preferred_element_type=jnp.float32
+        )
+    intensity_ref[...] = jnp.exp(log_rate)
+
+
+def forward(covariates, w_in, b_in, w_out, b_out):
+    rows, cov = covariates.shape
+    hid, species = w_out.shape
+    block = 512
+    return pl.pallas_call(
+        forward_kernel,
+        grid=(rows // block,),
+        out_shape=jax.ShapeDtypeStruct((rows, species), jnp.float32),
+        in_specs=[
+            pl.BlockSpec((block, cov), lambda i: (i, 0)),
+            pl.BlockSpec((cov, hid), lambda i: (0, 0)),
+            pl.BlockSpec((1, hid), lambda i: (0, 0)),
+            pl.BlockSpec((hid, species), lambda i: (0, 0)),
+            pl.BlockSpec((1, species), lambda i: (0, 0)),
+        ],
+        out_specs=pl.BlockSpec((block, species), lambda i: (i, 0)),
+        compiler_params=pltpu.CompilerParams(vmem_limit_bytes=VMEM_LIMIT),
+        name="habitat_forward",
+    )(covariates, w_in, b_in.reshape(1, hid), w_out, b_out.reshape(1, species))
+
+
+def backward_kernel(x_ref, w_in_ref, b_in_ref, w_out_ref, dlog_ref, gin_ref, gout_ref, turned):
+    step = pl.program_id(0)
+
+    @pl.when(step == 0)
+    def _():
+        gin_ref[...] = jnp.zeros_like(gin_ref)
+        turned[...] = jnp.zeros_like(turned)
+
+    x = x_ref[...]
+    dlog = dlog_ref[...]
+    hidden_units = w_in_ref.shape[1]
+    for c in range(0, hidden_units, 512):
+        pre = jnp.dot(x, w_in_ref[:, c : c + 512], preferred_element_type=jnp.float32)
+        pre = pre + b_in_ref[:, c : c + 512]
+        sig = sigmoid(pre)
+        act = pre * sig
+        back = lax.dot_general(
+            dlog,
+            w_out_ref[c : c + 512, :],
+            (((1,), (1,)), ((), ())),
+            preferred_element_type=jnp.float32,
+        )
+        dpre = (back * (sig + act * (1.0 - sig))).astype(jnp.bfloat16)
+        gin_ref[:, c : c + 512] += lax.dot_general(
+            x, dpre, (((0,), (0,)), ((), ())), preferred_element_type=jnp.float32
+        )
+        turned[:, c : c + 512] += lax.dot_general(
+            dlog,
+            act.astype(jnp.bfloat16),
+            (((0,), (0,)), ((), ())),
+            preferred_element_type=jnp.float32,
+        )
+
+    @pl.when(step == pl.num_programs(0) - 1)
+    def _():
+        gout_ref[...] = turned[...].T
+
+
+def backward(covariates, w_in, b_in, w_out, dlog):
+    rows, cov = covariates.shape
+    hid, species = w_out.shape
+    block = 512
+    return pl.pallas_call(
+        backward_kernel,
+        grid=(rows // block,),
+        out_shape=(
+            jax.ShapeDtypeStruct((cov, hid), jnp.float32),
+            jax.ShapeDtypeStruct((hid, species), jnp.float32),
+        ),
+        in_specs=[
+            pl.BlockSpec((block, cov), lambda i: (i, 0)),
+            pl.BlockSpec((cov, hid), lambda i: (0, 0)),
+            pl.BlockSpec((1, hid), lambda i: (0, 0)),
+            pl.BlockSpec((hid, species), lambda i: (0, 0)),
+            pl.BlockSpec((block, species), lambda i: (i, 0)),
+        ],
+        out_specs=(
+            pl.BlockSpec((cov, hid), lambda i: (0, 0)),
+            pl.BlockSpec((hid, species), lambda i: (0, 0)),
+        ),
+        scratch_shapes=[pltpu.VMEM((species, hid), jnp.float32)],
+        compiler_params=pltpu.CompilerParams(vmem_limit_bytes=VMEM_LIMIT),
+        name="habitat_backward",
+    )(covariates, w_in, b_in.reshape(1, hid), w_out, dlog)
+
+
+def iota(shape, dim):
+    return lax.broadcasted_iota(jnp.int32, shape, dim)
+
+
+def onehot(mask):
+    return jnp.where(mask, 1.0, 0.0).astype(jnp.bfloat16)
+
+
+def pack_kernel(slots, owner_ref, cell_ref, intensity_ref, send_ref, slot_ref, rows_ref, hot, wide):
+    rows = owner_ref.shape[0]
+    devices = send_ref.shape[0]
+    chunk = 256
+    below = onehot(iota((chunk, chunk), 0) > iota((chunk, chunk), 1))
+    lane = iota((chunk, 128), 1)
+    seen = jnp.zeros((1, 128), jnp.float32)
+    for c in range(0, rows, chunk):
+        owner = owner_ref[c : c + chunk, :]
+        named = owner == lane
+        hot_c = onehot(named)
+        before = jnp.dot(below, hot_c, preferred_element_type=jnp.float32) + seen
+        place = jnp.sum(jnp.where(named, before, 0.0), axis=1, keepdims=True)
+        seen = seen + jnp.sum(jnp.where(named, 1.0, 0.0), axis=0, keepdims=True)
+        flat = owner * slots + place.astype(jnp.int32)
+        spread = jnp.broadcast_to(flat, (chunk, 128))
+        slot_ref[c : c + chunk, :] = spread
+        for h in range(0, chunk, 128):
+            turned = spread[h : h + 128, :].astype(jnp.float32).T
+            rows_ref[pl.ds((c + h) // 128, 1), :] = turned[0:1, :].astype(jnp.int32)
+        cell = jnp.broadcast_to(cell_ref[c : c + chunk, :], (chunk, 128))
+        high = cell // 128
+        coded = jnp.where(lane == 0, high, jnp.where(lane == 1, cell - high * 128, 0))
+        wide[c : c + chunk, 0:128] = intensity_ref[c : c + chunk, :].astype(jnp.bfloat16)
+        wide[c : c + chunk, 128:256] = coded.astype(jnp.float32).astype(jnp.bfloat16)
+
+    block = hot.shape[0]
+    per_block = block // slots
+
+    def step(m, _):
+        row_id = iota((block, 128), 0) + m * block
+        for j in range(rows // 128):
+            hot[:, 128 * j : 128 * j + 128] = onehot(row_id == rows_ref[pl.ds(j, 1), :])
+        packed = jnp.dot(hot[...], wide[...], preferred_element_type=jnp.float32)
+        for q in range(per_block):
+            part = packed[q * slots : (q + 1) * slots]
+            target = m * per_block + q
+            send_ref[target, 0:slots, :] = part[:, 0:128].astype(jnp.bfloat16)
+            turned = part[:, 128:256].T[0:16]
+            if slots < 128:
+                turned = jnp.concatenate(
+                    [turned, jnp.zeros((16, 128 - slots), jnp.float32)], axis=1
+                )
+            send_ref[target, slots : slots + 16, :] = turned.astype(jnp.bfloat16)
+        return 0
+
+    lax.fori_loop(0, devices // per_block, step, 0)
+
+
+def pack(owner, land_cell, intensity, devices, slots):
+    rows, species = intensity.shape
+    block = min(1024, devices * slots)
+    return local_call(
+        functools.partial(pack_kernel, slots),
+        (
+            jax.ShapeDtypeStruct((devices, slots + 16, species), jnp.bfloat16),
+            jax.ShapeDtypeStruct((rows, 128), jnp.int32),
+        ),
+        (owner, land_cell.reshape(rows, 1), intensity),
+        scratch=(
+            pltpu.VMEM((rows // 128, 128), jnp.int32),
+            pltpu.VMEM((block, rows), jnp.bfloat16),
+            pltpu.VMEM((rows, 256), jnp.bfloat16),
+        ),
+        name="pack",
+    )
+
+
+def cell_row(got_ref, d, slots):
+    coded = got_ref[d, slots : slots + 16, :].astype(jnp.float32)
+    return (coded[0:1, :] * 128.0 + coded[1:2, :]).astype(jnp.int32)
+
+
+def place_kernel(slots, got_ref, start_ref, hot):
+    devices = got_ref.shape[0]
+    cells, block = hot.shape
+    per_block = block // slots
+    start_ref[...] = jnp.full(start_ref.shape, 0.1, jnp.float32)
+
+    def step(m, _):
+        for q in range(per_block):
+            row = cell_row(got_ref, m * per_block + q, slots)
+            mask = iota((cells, slots), 0) == row[:, 0:slots]
+            hot[:, q * slots : (q + 1) * slots] = onehot(mask)
+        values = got_ref[pl.ds(m * per_block, per_block), 0:slots, :].reshape(block, 128)
+        start_ref[...] += jnp.dot(hot[...], values, preferred_element_type=jnp.float32)
+        return 0
+
+    lax.fori_loop(0, devices // per_block, step, 0)
+
+
+def place(got, slots, cells):
+    devices, _, species = got.shape
+    block = min(1024, devices * slots)
+    return local_call(
+        functools.partial(place_kernel, slots),
+        jax.ShapeDtypeStruct((cells, species), jnp.float32),
+        (got,),
+        scratch=(pltpu.VMEM((cells, block), jnp.bfloat16),),
+        name="place",
+    )
+
+
+def collect_kernel(slots, got_ref, grad_ref, back_ref, hot, narrow):
+    devices = got_ref.shape[0]
+    block, cells = hot.shape
+    per_block = block // slots
+    narrow[...] = grad_ref[...].astype(jnp.bfloat16)
+
+    def step(m, _):
+        for q in range(per_block):
+            row = cell_row(got_ref, m * per_block + q, slots)
+            spread = jnp.broadcast_to(row.astype(jnp.float32), (128, 128)).T[0:slots]
+            column = spread.astype(jnp.int32)
+            for j in range(cells // 128):
+                hot[q * slots : (q + 1) * slots, 128 * j : 128 * j + 128] = onehot(
+                    column == iota((slots, 128), 1) + 128 * j
+                )
+        found = jnp.dot(hot[...], narrow[...], preferred_element_type=jnp.float32)
+        back_ref[pl.ds(m * per_block, per_block)] = found.astype(jnp.bfloat16).reshape(
+            per_block, slots, 128
+        )
+        return 0
+
+    lax.fori_loop(0, devices // per_block, step, 0)
+
+
+def collect(got, grad_field, slots):
+    devices, _, species = got.shape
+    cells = grad_field.shape[0]
+    block = min(1024, devices * slots)
+    return local_call(
+        functools.partial(collect_kernel, slots),
+        jax.ShapeDtypeStruct((devices, slots, species), jnp.bfloat16),
+        (got, grad_field),
+        scratch=(
+            pltpu.VMEM((block, cells), jnp.bfloat16),
+            pltpu.VMEM((cells, species), jnp.bfloat16),
+        ),
+        name="collect",
+    )
+
+
+def unpack_kernel(home_ref, slot_ref, intensity_ref, dlog_ref, hot):
+    block, total = hot.shape
+    rows = slot_ref.shape[0]
+
+    def step(m, _):
+        span = pl.ds(pl.multiple_of(m * block, block), block)
+        for j in range(total // 128):
+            hot[:, 128 * j : 128 * j + 128] = onehot(
+                slot_ref[span, :] == iota((block, 128), 1) + 128 * j
+            )
+        returned = jnp.dot(hot[...], home_ref[...], preferred_element_type=jnp.float32)
+        dlog_ref[span, :] = (returned * intensity_ref[span, :]).astype(jnp.bfloat16)
+        return 0
+
+    lax.fori_loop(0, rows // block, step, 0)
+
+
+def unpack(home, slot, intensity):
+    rows, species = intensity.shape
+    return local_call(
+        unpack_kernel,
+        jax.ShapeDtypeStruct((rows, species), jnp.bfloat16),
+        (home, slot, intensity),
+        scratch=(pltpu.VMEM((512, home.shape[0]), jnp.bfloat16),),
+        name="unpack",
+    )
+
+
 def normalize(taps):
     return taps / jnp.sum(taps, axis=1, keepdims=True)
-
-
-def silu_slope(value):
-    sigmoid_v = jax.nn.sigmoid(value)
-    return sigmoid_v + value * sigmoid_v * (1.0 - sigmoid_v)
 
 
 def local(
@@ -438,77 +732,21 @@
     slot_count = 2 * row_count // devices
     height, tile_width, species = observed.shape
     cell_count = height * tile_width
-    preact = jnp.dot(covariates, w_in, preferred_element_type=jnp.float32) + b_in
-    hidden = jax.nn.silu(preact).astype(jnp.bfloat16)
-    log_rate = jnp.dot(hidden, w_out, preferred_element_type=jnp.float32) + b_out
-    intensity = jnp.exp(log_rate)
-    sent = intensity.astype(jnp.bfloat16)
-    owner_rows = owner[:, 0]
-    onehot = (owner_rows[:, None] == jnp.arange(devices, dtype=jnp.int32)[None, :]).astype(
-        jnp.int32
-    )
-    before = jnp.cumsum(onehot, axis=0) - onehot
-    slot_idx = jnp.sum(before * onehot, axis=1)
-    flat_slot = owner_rows * slot_count + slot_idx
-    send_values = jnp.zeros((devices * slot_count, species), jnp.bfloat16).at[flat_slot].set(sent)
-    send_cells = (
-        jnp.full((devices * slot_count,), cell_count, jnp.int32).at[flat_slot].set(land_cell)
-    )
-    got_values, got_cells = (
-        lax.all_to_all(
-            send_values.reshape(devices, slot_count, species),
-            ("ty", "tx"),
-            split_axis=0,
-            concat_axis=0,
-            tiled=True,
-        ),
-        lax.all_to_all(
-            send_cells.reshape(devices, slot_count),
-            ("ty", "tx"),
-            split_axis=0,
-            concat_axis=0,
-            tiled=True,
-        ),
-    )
-    cell_list = got_cells.reshape(-1)
-    start_field = (
-        jnp.zeros((cell_count, species), jnp.float32)
-        .at[cell_list]
-        .add(got_values.reshape(-1, species).astype(jnp.float32), mode="drop")
-    )
-    field = 0.1 + start_field.reshape(height, tile_width, species)
+    intensity = forward(covariates, w_in, b_in, w_out, b_out)
+    send, slot = pack(owner, land_cell, intensity, devices, slot_count)
+    got = lax.all_to_all(send, ("ty", "tx"), split_axis=0, concat_axis=0, tiled=True)
+    start = place(got, slot_count, cell_count).reshape(height, tile_width, species)
     taps_y = normalize(row_taps)
     taps_x = normalize(col_taps)
-    scale = 1.0 / math.sqrt(row_count * devices)
-    seen = surveyed.astype(jnp.float32) * scale
+    seen = surveyed.astype(jnp.float32) * (1.0 / math.sqrt(row_count * devices))
     field, grad_field = raster_steps(
-        field, taps_y, taps_x, rate, capacity, observed, seen, tiles_y, tiles_x
-    )
-    back_values = jnp.take(
-        grad_field.reshape(cell_count, species), cell_list, axis=0, mode="fill", fill_value=0.0
-    ).astype(jnp.bfloat16)
-    home_values = lax.all_to_all(
-        back_values.reshape(devices, slot_count, species),
-        ("ty", "tx"),
-        split_axis=0,
-        concat_axis=0,
-        tiled=True,
-    )
-    returned = home_values.reshape(devices * slot_count, species)[flat_slot]
-    dlog = (returned.astype(jnp.float32) * intensity).astype(jnp.bfloat16)
-    dhidden = lax.dot_general(
-        dlog, w_out, (((1,), (1,)), ((), ())), preferred_element_type=jnp.float32
-    )
-    dpre = (dhidden * silu_slope(preact)).astype(jnp.bfloat16)
+        start, taps_y, taps_x, rate, capacity, observed, seen, tiles_y, tiles_x
+    )
+    back = collect(got, grad_field.reshape(cell_count, species), slot_count)
+    home = lax.all_to_all(back, ("ty", "tx"), split_axis=0, concat_axis=0, tiled=True)
+    dlog = unpack(home.reshape(devices * slot_count, species), slot, intensity)
     grad_w_in, grad_w_out = sum_grads(
-        lax.dot_general(
-            covariates, dpre, (((0,), (0,)), ((), ())), preferred_element_type=jnp.float32
-        ),
-        lax.dot_general(
-            hidden, dlog, (((0,), (0,)), ((), ())), preferred_element_type=jnp.float32
-        ),
-        tiles_y,
-        tiles_x,
+        *backward(covariates, w_in, b_in, w_out, dlog), tiles_y, tiles_x
     )
     return (field, grad_w_in, grad_w_out)
 

time: 295 us -> 250 us (0.85)
  Pallas kernels: 96.9 us -> 169 us
  other arithmetic: 45.6 us -> 0.65 us
  matrix products: 36.5 us -> 0 us
  local copies, waits for them, and re-layouts: 41.2 us -> 9.6 us
  starting transfers between devices: 18.8 us -> 12.5 us
    pallas_call x0 -> x6, Pallas kernels: none -> 71.6 us  [the longest x4 39.6 us: local_call(): pl.pallas_call(body, out_shape=shapes, in_specs=[vmem] * len(args), out_s...]
    dot_general x5 -> x0, matrix products: 36.5 us -> none  [the longest x1 10.7 us: local(): jnp.dot(covariates, w_in, preferred_element_type=jnp.float32) + b_in]
    scatter-add x1 -> x0, other arithmetic: 23.7 us -> none  [local(): start_field = jnp.zeros((cell_count, species), jnp.float32).at[cell_list]...]
    gather x2 -> x0, local copies, waits for them, and re-layouts: 23.6 us -> none  [the longest x1 15.6 us: local(): jnp.take(grad_field.reshape(cell_count, species), cell_list, axis=0, mode...]
    another operation x3 -> x0, other arithmetic: 9.41 us -> none
    scatter x1 -> x0, local copies, waits for them, and re-layouts: 8.79 us -> none  [local(): jnp.full((devices * slot_count,), cell_count, jnp.int32).at[flat_slot]]
    scatter x1 -> x0, other arithmetic: 6.78 us -> none  [local(): jnp.zeros((devices * slot_count, species), jnp.bfloat16).at[flat_slot]]
    all_to_all x3 -> x2, starting transfers between devices: 18.8 us -> 12.5 us  [the longest x1 7.3 us: local(): lax.all_to_all(send, ('ty', 'tx'), split_axis=0, concat_axis=0, tiled=True)]
  transfers between devices with their start and end apart: 3 -> 2, of which waited for: 2 -> 2; matrix products, arithmetic and copies ran while one was open for 7% -> 0% of each run, Pallas kernels for 0% -> 0%
where the time goes in v2:
time: 250 us
  Pallas kernels  169 us (68%)
  waiting for transfers between devices  57.3 us (23%)
  starting transfers between devices  12.5 us (5%)
  local copies, waits for them, and re-layouts  9.6 us (4%)
    pallas_call x1, Pallas kernels, raster_steps(): pl.pallas_call(functools.partial(raster_kernel, tiles_y, tiles_x), out_sh...  56.1 us
    pallas_call x1, Pallas kernels, sum_grads(): pl.pallas_call(functools.partial(sum_kernel, tiles_y, tiles_x, plan), out...  41.1 us
    pallas_call x4, Pallas kernels, local_call(): pl.pallas_call(body, out_shape=shapes, in_specs=[vmem] * len(args), out_s...  39.6 us
    all_to_all x1, waiting for transfers between devices, local(): lax.all_to_all(send, ('ty', 'tx'), split_axis=0, concat_axis=0, tiled=True)  29.7 us
    all_to_all x1, waiting for transfers between devices, local(): lax.all_to_all(back, ('ty', 'tx'), split_axis=0, concat_axis=0, tiled=True)  27.6 us
    pallas_call x1, Pallas kernels, backward(): pl.pallas_call(backward_kernel, grid=(rows // block,), out_shape=(jax.Sha...  20.4 us
    pallas_call x1, Pallas kernels, forward(): pl.pallas_call(forward_kernel, grid=(rows // block,), out_shape=jax.Shape...  11.6 us
    all_to_all x1, starting transfers between devices, local(): lax.all_to_all(send, ('ty', 'tx'), split_axis=0, concat_axis=0, tiled=True)  7.3 us
  transfers between devices with their start and end apart: 2, of which 2 were waited for; matrix products, arithmetic and copies ran while one was open for 0% of the time, Pallas kernels for 0%

profile of v2, /device:TPU:0, one launch (start us, length us, event | category | flops | bytes accessed | tf_op | source)
XLA Modules:
  0.0 249.5 jit_solution(7822774988349516971)
XLA Ops:
  0.6 2.0 copy.17.owner_ref
  2.7 2.1 copy.18.cell_ref
  4.7 11.6 %habitat_forward.1.intensity_ref = f32[2048,128]{1,0:T(8,128)} custom-call(bf16[2048,512]{1,0:T(8,128)(2,1)} %x_ref.3, bf16[512,2048]{1,0:T(8,128)(2,1)} %w_in_ref.3, f32[1,2048]{1,0:T(1,128)} %bitcast.19, bf16[2048,128]{1,0:T(8,128)(2,1)} %w_out_ref.3, f32[1,128]{1,0:T(1,128)} %bitcast.22), custom_call_target="tpu_custom_call" | custom-call | tf_op jit(solution)/shard_map/habitat_forward/pallas_call | solution.py:447
  16.3 12.4 %pack.1 = (bf16[32,144,128]{2,1,0:T(8,128)(2,1)}, s32[2048,128]{1,0:T(8,128)}) custom-call(s32[2048,1]{1,0:T(8,128)} %copy.17.owner_ref, s32[2048,1]{1,0:T(8,128)} %copy.18.cell_ref, f32[2048,128]{1,0:T(8,128)} %habitat_forward.1.intensity_ref), custom_call_target="tpu_custom_call" | custom-call | tf_op jit(solution)/shard_map/pack/pallas_call | solution.py:413
  28.8 7.3 %all-to-all-start = ((bf16[32,144,128]{2,1,0:T(8,128)(2,1)}), bf16[32,144,128]{2,1,0:T(8,128)(2,1)S(1)}, u32[]{:S(2)}, u32[]{:S(2)}) async-start(bf16[32,144,128]{2,1,0:T(8,128)(2,1)} %get-tuple-element.11), calls=%async_computation | async-start | bytes 2359296 | tf_op jit(solution)/shard_map/all_to_all | solution.py:737
  36.1 0.0 copy-done.6
  36.1 0.0 copy-done.5
  36.1 0.6 convert_multiply_fusion.sur_ref
  36.7 29.7 %all-to-all-done.got_ref = bf16[32,144,128]{2,1,0:T(8,128)(2,1)S(1)} async-done(((bf16[32,144,128]{2,1,0:T(8,128)(2,1)}), bf16[32,144,128]{2,1,0:T(8,128)(2,1)S(1)}, u32[]{:S(2)}, u32[]{:S(2)}) %all-to-all-start) | async-done | bytes 1179680 | tf_op jit(solution)/shard_map/all_to_all | solution.py:737
  66.5 1.0 copy-done
  67.5 10.0 %place.1 = f32[2048,128]{1,0:T(8,128)} custom-call(bf16[32,144,128]{2,1,0:T(8,128)(2,1)} %copy-done), custom_call_target="tpu_custom_call" | custom-call | tf_op jit(solution)/shard_map/place/pallas_call | solution.py:413
  77.4 0.6 broadcast_in_dim.4.taps_y_ref
  78.1 0.6 broadcast_in_dim.5.taps_x_ref
  78.7 56.1 %raster_steps.1 = (f32[16,128,128]{2,1,0:T(8,128)}, f32[16,128,128]{2,1,0:T(8,128)}) custom-call(f32[16,128,128]{2,1,0:T(8,128)} %bitcast.16, f32[9,8,128]{2,1,0:T(8,128)} %broadcast_in_dim.4.taps_y_ref, f32[9,8,128]{2,1,0:T(8,128)} %broadcast_in_dim.5.taps_x_ref, f32[1,128]{1,0:T(1,128)} %bitcast.23, f32[1,128]{1,0:T(1,128)} %bitcast.24, ...), custom_call_target="tpu_custom_call" | custom-call | tf_op jit(solution)/shard_map/raster_steps/pallas_call | solution.py:381
  134.8 9.2 %collect.1 = bf16[32,128,128]{2,1,0:T(8,128)(2,1)} custom-call(bf16[32,144,128]{2,1,0:T(8,128)(2,1)} %copy-done, f32[2048,128]{1,0:T(8,128)} %bitcast.17), custom_call_target="tpu_custom_call" | custom-call | tf_op jit(solution)/shard_map/collect/pallas_call | solution.py:413
  143.9 5.3 %all-to-all-start.1 = ((bf16[32,128,128]{2,1,0:T(8,128)(2,1)}), bf16[32,128,128]{2,1,0:T(8,128)(2,1)S(1)}, u32[]{:S(2)}, u32[]{:S(2)}) async-start(bf16[32,128,128]{2,1,0:T(8,128)(2,1)} %collect.1), calls=%async_computation.1 | async-start | bytes 2097152 | tf_op jit(solution)/shard_map/all_to_all | solution.py:746
  149.2 27.6 %all-to-all-done.1 = bf16[32,128,128]{2,1,0:T(8,128)(2,1)S(1)} async-done(((bf16[32,128,128]{2,1,0:T(8,128)(2,1)}), bf16[32,128,128]{2,1,0:T(8,128)(2,1)S(1)}, u32[]{:S(2)}, u32[]{:S(2)}) %all-to-all-start.1) | async-done | bytes 1048608 | tf_op jit(solution)/shard_map/all_to_all | solution.py:746
  176.8 1.0 copy-done.1
  177.7 8.0 %unpack.1.dlog_ref = bf16[2048,128]{1,0:T(8,128)(2,1)} custom-call(bf16[4096,128]{1,0:T(8,128)(2,1)} %bitcast.15, s32[2048,128]{1,0:T(8,128)} %get-tuple-element.14.slot_ref, f32[2048,128]{1,0:T(8,128)} %habitat_forward.1.intensity_ref), custom_call_target="tpu_custom_call" | custom-call | tf_op jit(solution)/shard_map/unpack/pallas_call | solution.py:413
  185.8 20.4 %habitat_backward.1 = (f32[512,2048]{1,0:T(8,128)}, f32[2048,128]{1,0:T(8,128)}) custom-call(bf16[2048,512]{1,0:T(8,128)(2,1)} %x_ref.3, bf16[512,2048]{1,0:T(8,128)(2,1)} %w_in_ref.3, f32[1,2048]{1,0:T(1,128)} %bitcast.20, bf16[2048,128]{1,0:T(8,128)(2,1)} %w_out_ref.3, bf16[2048,128]{1,0:T(8,128)(2,1)} %unpack.1.dlog_ref), custom_call_target="tpu_custom_call" | custom-call | tf_op jit(solution)/shard_map/habitat_backward/pallas_call | solution.py:506
  206.2 41.1 %sum_grads.1 = (f32[16,2048]{1,0:T(8,128)}, f32[64,128]{1,0:T(8,128)}) custom-call(f32[2,2,8,16,2048]{4,3,2,1,0:T(8,128)} %bitcast.14, f32[2,2,8,64,128]{4,3,2,1,0:T(8,128)} %bitcast.18), custom_call_target="tpu_custom_call" | custom-call | tf_op jit(solution)/shard_map/sum_grads/pallas_call | solution.py:145
  247.3 1.0 copy.22
  248.3 0.7 copy.23
  248.9 0.6 copy.24
  (16 shorter events, 0.1 us)
Async XLA Ops:
  16.3 19.8 %copy-start.6 = (f32[128,9]{0,1:T(8,128)S(1)}, f32[128,9]{0,1:T(8,128)}, u32[]{:S(2)}) copy-start(f32[128,9]{0,1:T(8,128)} %param.20) | copy-start | bytes 13828
  16.3 19.8 %copy-start.5 = (f32[128,9]{0,1:T(8,128)S(1)}, f32[128,9]{0,1:T(8,128)}, u32[]{:S(2)}) copy-start(f32[128,9]{0,1:T(8,128)} %param.21) | copy-start | bytes 13828
  16.3 19.8 %copy-start.7 = (s32[16,128]{1,0:T(8,128)S(1)}, s32[16,128]{1,0:T(8,128)}, u32[]{:S(2)}) copy-start(s32[16,128]{1,0:T(8,128)} %param.25) | copy-start | bytes 24580
  28.8 37.7 %all-to-all-start = ((bf16[32,144,128]{2,1,0:T(8,128)(2,1)}), bf16[32,144,128]{2,1,0:T(8,128)(2,1)S(1)}, u32[]{:S(2)}, u32[]{:S(2)}) async-start(bf16[32,144,128]{2,1,0:T(8,128)(2,1)} %get-tuple-element.11), calls=%async_computation | async-start | bytes 2359296 | tf_op jit(solution)/shard_map/all_to_all | solution.py:737
  66.5 1.0 copy-start
  143.9 32.8 %all-to-all-start.1 = ((bf16[32,128,128]{2,1,0:T(8,128)(2,1)}), bf16[32,128,128]{2,1,0:T(8,128)(2,1)S(1)}, u32[]{:S(2)}, u32[]{:S(2)}) async-start(bf16[32,128,128]{2,1,0:T(8,128)(2,1)} %collect.1), calls=%async_computation.1 | async-start | bytes 2097152 | tf_op jit(solution)/shard_map/all_to_all | solution.py:746
  176.8 1.0 copy-start.1
  206.2 41.1 %copy-start.2 = (f32[16,128,128]{2,1,0:T(8,128)S(1)}, f32[16,128,128]{2,1,0:T(8,128)}, u32[]{:S(2)}) copy-start(f32[16,128,128]{2,1,0:T(8,128)} %get-tuple-element.22) | copy-start | bytes 3145732
  247.3 1.0 copy-start.3
  247.3 1.7 copy-start.4

commit v3 on v2

--- a/solution.py
+++ b/solution.py
@@ -461,7 +461,43 @@
     )(covariates, w_in, b_in.reshape(1, hid), w_out, b_out.reshape(1, species))
 
 
-def backward_kernel(x_ref, w_in_ref, b_in_ref, w_out_ref, dlog_ref, gin_ref, gout_ref, turned):
+def prepare_kernel(x_ref, w_in_ref, b_in_ref, hidden_ref, slope_ref):
+    x = x_ref[...]
+    for c in range(0, w_in_ref.shape[1], 512):
+        pre = jnp.dot(x, w_in_ref[:, c : c + 512], preferred_element_type=jnp.float32)
+        pre = pre + b_in_ref[:, c : c + 512]
+        sig = sigmoid(pre)
+        act = pre * sig
+        hidden_ref[:, c : c + 512] = act.astype(jnp.bfloat16)
+        slope_ref[:, c : c + 512] = sig + act * (1.0 - sig)
+
+
+def prepare(covariates, w_in, b_in):
+    rows, cov = covariates.shape
+    hid = w_in.shape[1]
+    block = 512
+    return pl.pallas_call(
+        prepare_kernel,
+        grid=(rows // block,),
+        out_shape=(
+            jax.ShapeDtypeStruct((rows, hid), jnp.bfloat16),
+            jax.ShapeDtypeStruct((rows, hid), jnp.float32),
+        ),
+        in_specs=[
+            pl.BlockSpec((block, cov), lambda i: (i, 0)),
+            pl.BlockSpec((cov, hid), lambda i: (0, 0)),
+            pl.BlockSpec((1, hid), lambda i: (0, 0)),
+        ],
+        out_specs=(pl.BlockSpec((block, hid), lambda i: (i, 0)),) * 2,
+        compiler_params=pltpu.CompilerParams(vmem_limit_bytes=VMEM_LIMIT),
+        cost_estimate=pl.CostEstimate(
+            flops=2 * rows * cov * hid, bytes_accessed=8 * rows * hid, transcendentals=rows * hid
+        ),
+        name="habitat_prepare",
+    )(covariates, w_in, b_in.reshape(1, hid))
+
+
+def backward_kernel(x_ref, w_out_ref, dlog_ref, hidden_ref, slope_ref, gin_ref, gout_ref, turned):
     step = pl.program_id(0)
 
     @pl.when(step == 0)
@@ -471,25 +507,20 @@
 
     x = x_ref[...]
     dlog = dlog_ref[...]
-    hidden_units = w_in_ref.shape[1]
-    for c in range(0, hidden_units, 512):
-        pre = jnp.dot(x, w_in_ref[:, c : c + 512], preferred_element_type=jnp.float32)
-        pre = pre + b_in_ref[:, c : c + 512]
-        sig = sigmoid(pre)
-        act = pre * sig
+    for c in range(0, w_out_ref.shape[0], 512):
         back = lax.dot_general(
             dlog,
             w_out_ref[c : c + 512, :],
             (((1,), (1,)), ((), ())),
             preferred_element_type=jnp.float32,
         )
-        dpre = (back * (sig + act * (1.0 - sig))).astype(jnp.bfloat16)
+        dpre = (back * slope_ref[:, c : c + 512]).astype(jnp.bfloat16)
         gin_ref[:, c : c + 512] += lax.dot_general(
             x, dpre, (((0,), (0,)), ((), ())), preferred_element_type=jnp.float32
         )
         turned[:, c : c + 512] += lax.dot_general(
             dlog,
-            act.astype(jnp.bfloat16),
+            hidden_ref[:, c : c + 512],
             (((0,), (0,)), ((), ())),
             preferred_element_type=jnp.float32,
         )
@@ -499,7 +530,7 @@
         gout_ref[...] = turned[...].T
 
 
-def backward(covariates, w_in, b_in, w_out, dlog):
+def backward(covariates, w_out, dlog, hidden, slope):
     rows, cov = covariates.shape
     hid, species = w_out.shape
     block = 512
@@ -512,10 +543,10 @@
         ),
         in_specs=[
             pl.BlockSpec((block, cov), lambda i: (i, 0)),
-            pl.BlockSpec((cov, hid), lambda i: (0, 0)),
-            pl.BlockSpec((1, hid), lambda i: (0, 0)),
             pl.BlockSpec((hid, species), lambda i: (0, 0)),
             pl.BlockSpec((block, species), lambda i: (i, 0)),
+            pl.BlockSpec((block, hid), lambda i: (i, 0)),
+            pl.BlockSpec((block, hid), lambda i: (i, 0)),
         ],
         out_specs=(
             pl.BlockSpec((cov, hid), lambda i: (0, 0)),
@@ -524,7 +555,7 @@
         scratch_shapes=[pltpu.VMEM((species, hid), jnp.float32)],
         compiler_params=pltpu.CompilerParams(vmem_limit_bytes=VMEM_LIMIT),
         name="habitat_backward",
-    )(covariates, w_in, b_in.reshape(1, hid), w_out, dlog)
+    )(covariates, w_out, dlog, hidden, slope)
 
 
 def iota(shape, dim):
@@ -535,27 +566,35 @@
     return jnp.where(mask, 1.0, 0.0).astype(jnp.bfloat16)
 
 
+def column(ref, first, count):
+    tiles = []
+    for r in range(first // 128, (first + count) // 128):
+        row = ref[r : r + 1, :].astype(jnp.float32)
+        tiles.append(jnp.broadcast_to(row, (128, 128)).T)
+    return jnp.concatenate(tiles, axis=0).astype(jnp.int32)
+
+
 def pack_kernel(slots, owner_ref, cell_ref, intensity_ref, send_ref, slot_ref, rows_ref, hot, wide):
-    rows = owner_ref.shape[0]
+    rows = intensity_ref.shape[0]
     devices = send_ref.shape[0]
     chunk = 256
     below = onehot(iota((chunk, chunk), 0) > iota((chunk, chunk), 1))
     lane = iota((chunk, 128), 1)
     seen = jnp.zeros((1, 128), jnp.float32)
     for c in range(0, rows, chunk):
-        owner = owner_ref[c : c + chunk, :]
+        owner = column(owner_ref, c, chunk)
         named = owner == lane
         hot_c = onehot(named)
         before = jnp.dot(below, hot_c, preferred_element_type=jnp.float32) + seen
         place = jnp.sum(jnp.where(named, before, 0.0), axis=1, keepdims=True)
         seen = seen + jnp.sum(jnp.where(named, 1.0, 0.0), axis=0, keepdims=True)
         flat = owner * slots + place.astype(jnp.int32)
-        spread = jnp.broadcast_to(flat, (chunk, 128))
+        spread = flat
         slot_ref[c : c + chunk, :] = spread
         for h in range(0, chunk, 128):
             turned = spread[h : h + 128, :].astype(jnp.float32).T
             rows_ref[pl.ds((c + h) // 128, 1), :] = turned[0:1, :].astype(jnp.int32)
-        cell = jnp.broadcast_to(cell_ref[c : c + chunk, :], (chunk, 128))
+        cell = column(cell_ref, c, chunk)
         high = cell // 128
         coded = jnp.where(lane == 0, high, jnp.where(lane == 1, cell - high * 128, 0))
         wide[c : c + chunk, 0:128] = intensity_ref[c : c + chunk, :].astype(jnp.bfloat16)
@@ -593,7 +632,7 @@
             jax.ShapeDtypeStruct((devices, slots + 16, species), jnp.bfloat16),
             jax.ShapeDtypeStruct((rows, 128), jnp.int32),
         ),
-        (owner, land_cell.reshape(rows, 1), intensity),
+        (owner.reshape(rows // 128, 128), land_cell.reshape(rows // 128, 128), intensity),
         scratch=(
             pltpu.VMEM((rows // 128, 128), jnp.int32),
             pltpu.VMEM((block, rows), jnp.bfloat16),
@@ -734,7 +773,10 @@
     cell_count = height * tile_width
     intensity = forward(covariates, w_in, b_in, w_out, b_out)
     send, slot = pack(owner, land_cell, intensity, devices, slot_count)
+    bias, send = lax.optimization_barrier((b_in, send))
     got = lax.all_to_all(send, ("ty", "tx"), split_axis=0, concat_axis=0, tiled=True)
+    hidden, slope = prepare(covariates, w_in, bias)
+    got, hidden, slope = lax.optimization_barrier((got, hidden, slope))
     start = place(got, slot_count, cell_count).reshape(height, tile_width, species)
     taps_y = normalize(row_taps)
     taps_x = normalize(col_taps)
@@ -746,7 +788,7 @@
     home = lax.all_to_all(back, ("ty", "tx"), split_axis=0, concat_axis=0, tiled=True)
     dlog = unpack(home.reshape(devices * slot_count, species), slot, intensity)
     grad_w_in, grad_w_out = sum_grads(
-        *backward(covariates, w_in, b_in, w_out, dlog), tiles_y, tiles_x
+        *backward(covariates, w_out, dlog, hidden, slope), tiles_y, tiles_x
     )
     return (field, grad_w_in, grad_w_out)
 

time: 250 us -> 241 us (0.964)
  waiting for transfers between devices: 57.3 us -> 44.1 us
  Pallas kernels: 169 us -> 177 us
  local copies, waits for them, and re-layouts: 9.6 us -> 5.5 us
    all_to_all x1, waiting for transfers between devices: 29.7 us -> 16.5 us  [local(): lax.all_to_all(send, ('ty', 'tx'), split_axis=0, concat_axis=0, tiled=True)]
    pallas_call x0 -> x1, Pallas kernels: none -> 13.2 us  [prepare(): pl.pallas_call(prepare_kernel, grid=(rows // block,), out_shape=(jax.Shap...]
    pallas_call x1, Pallas kernels: 20.4 us -> 16.6 us  [backward(): pl.pallas_call(backward_kernel, grid=(rows // block,), out_shape=(jax.Sha...]
    unnamed x20 -> x19, local copies, waits for them, and re-layouts: 6.29 us -> 4.28 us
  transfers between devices with their start and end apart: 2 -> 2, of which waited for: 2 -> 2; matrix products, arithmetic and copies ran while one was open for 0% -> 0% of each run, Pallas kernels for 0% -> 5%
where the time goes in v3:
time: 241 us
  Pallas kernels  177 us (73%)
  waiting for transfers between devices  44.1 us (18%)
  starting transfers between devices  12.6 us (5%)
  local copies, waits for them, and re-layouts  5.5 us (2%)
    pallas_call x1, Pallas kernels, raster_steps(): pl.pallas_call(functools.partial(raster_kernel, tiles_y, tiles_x), out_sh...  56.1 us
    pallas_call x1, Pallas kernels, sum_grads(): pl.pallas_call(functools.partial(sum_kernel, tiles_y, tiles_x, plan), out...  41 us
    pallas_call x4, Pallas kernels, local_call(): pl.pallas_call(body, out_shape=shapes, in_specs=[vmem] * len(args), out_s...  38.7 us
    all_to_all x1, waiting for transfers between devices, local(): lax.all_to_all(back, ('ty', 'tx'), split_axis=0, concat_axis=0, tiled=True)  27.6 us
    pallas_call x1, Pallas kernels, backward(): pl.pallas_call(backward_kernel, grid=(rows // block,), out_shape=(jax.Sha...  16.6 us
    all_to_all x1, waiting for transfers between devices, local(): lax.all_to_all(send, ('ty', 'tx'), split_axis=0, concat_axis=0, tiled=True)  16.5 us
    pallas_call x1, Pallas kernels, prepare(): pl.pallas_call(prepare_kernel, grid=(rows // block,), out_shape=(jax.Shap...  13.2 us
    pallas_call x1, Pallas kernels, forward(): pl.pallas_call(forward_kernel, grid=(rows // block,), out_shape=jax.Shape...  11.6 us
  transfers between devices with their start and end apart: 2, of which 2 were waited for; matrix products, arithmetic and copies ran while one was open for 0% of the time, Pallas kernels for 5%

profile of v3, /device:TPU:0, one launch (start us, length us, event | category | flops | bytes accessed | tf_op | source)
XLA Modules:
  0.0 240.7 jit_solution(3002736155783465384)
XLA Ops:
  0.6 11.6 %habitat_forward.1.intensity_ref = f32[2048,128]{1,0:T(8,128)} custom-call(bf16[2048,512]{1,0:T(8,128)(2,1)} %x_ref.5, bf16[512,2048]{1,0:T(8,128)(2,1)} %w_in_ref.3, f32[1,2048]{1,0:T(1,128)} %bitcast.23, bf16[2048,128]{1,0:T(8,128)(2,1)} %w_out_ref.3, f32[1,128]{1,0:T(1,128)} %bitcast.25), custom_call_target="tpu_custom_call" | custom-call | tf_op jit(solution)/shard_map/habitat_forward/pallas_call | solution.py:447
  12.2 11.4 %pack.1 = (bf16[32,144,128]{2,1,0:T(8,128)(2,1)}, s32[2048,128]{1,0:T(8,128)}) custom-call(s32[16,128]{1,0:T(8,128)} %bitcast.21, s32[16,128]{1,0:T(8,128)} %bitcast.22, f32[2048,128]{1,0:T(8,128)} %habitat_forward.1.intensity_ref), custom_call_target="tpu_custom_call" | custom-call | tf_op jit(solution)/shard_map/pack/pallas_call | solution.py:413
  23.7 7.3 %all-to-all-start = ((bf16[32,144,128]{2,1,0:T(8,128)(2,1)}), bf16[32,144,128]{2,1,0:T(8,128)(2,1)S(1)}, u32[]{:S(2)}, u32[]{:S(2)}) async-start(bf16[32,144,128]{2,1,0:T(8,128)(2,1)} %get-tuple-element.19), calls=%async_computation | async-start | bytes 2359296 | tf_op jit(solution)/shard_map/all_to_all | solution.py:777
  31.0 0.6 convert_multiply_fusion.sur_ref
  31.6 13.2 %habitat_prepare.1 = (bf16[2048,2048]{1,0:T(8,128)(2,1)}, f32[2048,2048]{1,0:T(8,128)}) custom-call(bf16[2048,512]{1,0:T(8,128)(2,1)} %x_ref.5, bf16[512,2048]{1,0:T(8,128)(2,1)} %w_in_ref.3, f32[1,2048]{1,0:T(1,128)} %bitcast.24), custom_call_target="tpu_custom_call" | custom-call | flops 4294967296 | bytes 33554432 | tf_op jit(solution)/shard_map/habitat_prepare/pallas_call | solution.py:479
  44.8 16.5 %all-to-all-done.got_ref = bf16[32,144,128]{2,1,0:T(8,128)(2,1)S(1)} async-done(((bf16[32,144,128]{2,1,0:T(8,128)(2,1)}), bf16[32,144,128]{2,1,0:T(8,128)(2,1)S(1)}, u32[]{:S(2)}, u32[]{:S(2)}) %all-to-all-start) | async-done | bytes 1179680 | tf_op jit(solution)/shard_map/all_to_all | solution.py:777
  61.4 1.0 copy-done
  62.4 10.0 %place.1 = f32[2048,128]{1,0:T(8,128)} custom-call(bf16[32,144,128]{2,1,0:T(8,128)(2,1)} %copy-done), custom_call_target="tpu_custom_call" | custom-call | tf_op jit(solution)/shard_map/place/pallas_call | solution.py:413
  72.4 0.6 broadcast_in_dim.4.taps_y_ref
  73.0 0.6 broadcast_in_dim.5.taps_x_ref
  73.6 56.1 %raster_steps.1 = (f32[16,128,128]{2,1,0:T(8,128)}, f32[16,128,128]{2,1,0:T(8,128)}) custom-call(f32[16,128,128]{2,1,0:T(8,128)} %bitcast.18, f32[9,8,128]{2,1,0:T(8,128)} %broadcast_in_dim.4.taps_y_ref, f32[9,8,128]{2,1,0:T(8,128)} %broadcast_in_dim.5.taps_x_ref, f32[1,128]{1,0:T(1,128)} %bitcast.26, f32[1,128]{1,0:T(1,128)} %bitcast.27, ...), custom_call_target="tpu_custom_call" | custom-call | tf_op jit(solution)/shard_map/raster_steps/pallas_call | solution.py:381
  129.7 9.2 %collect.1 = bf16[32,128,128]{2,1,0:T(8,128)(2,1)} custom-call(bf16[32,144,128]{2,1,0:T(8,128)(2,1)} %copy-done, f32[2048,128]{1,0:T(8,128)} %bitcast.19), custom_call_target="tpu_custom_call" | custom-call | tf_op jit(solution)/shard_map/collect/pallas_call | solution.py:413
  138.9 5.3 %all-to-all-start.1 = ((bf16[32,128,128]{2,1,0:T(8,128)(2,1)}), bf16[32,128,128]{2,1,0:T(8,128)(2,1)S(1)}, u32[]{:S(2)}, u32[]{:S(2)}) async-start(bf16[32,128,128]{2,1,0:T(8,128)(2,1)} %collect.1), calls=%async_computation.1 | async-start | bytes 2097152 | tf_op jit(solution)/shard_map/all_to_all | solution.py:788
  144.2 27.6 %all-to-all-done.1 = bf16[32,128,128]{2,1,0:T(8,128)(2,1)S(1)} async-done(((bf16[32,128,128]{2,1,0:T(8,128)(2,1)}), bf16[32,128,128]{2,1,0:T(8,128)(2,1)S(1)}, u32[]{:S(2)}, u32[]{:S(2)}) %all-to-all-start.1) | async-done | bytes 1048608 | tf_op jit(solution)/shard_map/all_to_all | solution.py:788
  171.8 1.0 copy-done.1
  172.8 8.0 %unpack.1.dlog_ref = bf16[2048,128]{1,0:T(8,128)(2,1)} custom-call(bf16[4096,128]{1,0:T(8,128)(2,1)} %bitcast.17, s32[2048,128]{1,0:T(8,128)} %get-tuple-element.26.slot_ref, f32[2048,128]{1,0:T(8,128)} %habitat_forward.1.intensity_ref), custom_call_target="tpu_custom_call" | custom-call | tf_op jit(solution)/shard_map/unpack/pallas_call | solution.py:413
  180.7 16.6 %habitat_backward.1 = (f32[512,2048]{1,0:T(8,128)}, f32[2048,128]{1,0:T(8,128)}) custom-call(bf16[2048,512]{1,0:T(8,128)(2,1)} %x_ref.5, bf16[2048,128]{1,0:T(8,128)(2,1)} %w_out_ref.3, bf16[2048,128]{1,0:T(8,128)(2,1)} %unpack.1.dlog_ref, bf16[2048,2048]{1,0:T(8,128)(2,1)} %get-tuple-element.27.hidden_ref, f32[2048,2048]{1,0:T(8,128)} %get-tuple-element.28.slope_ref), custom_call_target="tpu_custom_call" | custom-call | tf_op jit(solution)/shard_map/habitat_backward/pallas_call | solution.py:537
  197.4 41.0 %sum_grads.1 = (f32[16,2048]{1,0:T(8,128)}, f32[64,128]{1,0:T(8,128)}) custom-call(f32[2,2,8,16,2048]{4,3,2,1,0:T(8,128)} %bitcast.16, f32[2,2,8,64,128]{4,3,2,1,0:T(8,128)} %bitcast.20), custom_call_target="tpu_custom_call" | custom-call | tf_op jit(solution)/shard_map/sum_grads/pallas_call | solution.py:145
  238.4 0.0 copy-start.3
  238.4 0.0 copy-start.4
  238.4 0.0 copy-done.2
  238.4 1.0 copy.19
  239.4 0.7 copy.20
  240.1 0.6 copy.21
  (15 shorter events, 0.1 us)
Async XLA Ops:
  12.2 18.8 %copy-start.6 = (f32[128,9]{0,1:T(8,128)S(1)}, f32[128,9]{0,1:T(8,128)}, u32[]{:S(2)}) copy-start(f32[128,9]{0,1:T(8,128)} %param.20) | copy-start | bytes 13828
  12.2 18.8 %copy-start.5 = (f32[128,9]{0,1:T(8,128)S(1)}, f32[128,9]{0,1:T(8,128)}, u32[]{:S(2)}) copy-start(f32[128,9]{0,1:T(8,128)} %param.21) | copy-start | bytes 13828
  12.2 18.8 %copy-start.7 = (s32[16,128]{1,0:T(8,128)S(1)}, s32[16,128]{1,0:T(8,128)}, u32[]{:S(2)}) copy-start(s32[16,128]{1,0:T(8,128)} %param.25) | copy-start | bytes 24580
  23.7 37.7 %all-to-all-start = ((bf16[32,144,128]{2,1,0:T(8,128)(2,1)}), bf16[32,144,128]{2,1,0:T(8,128)(2,1)S(1)}, u32[]{:S(2)}, u32[]{:S(2)}) async-start(bf16[32,144,128]{2,1,0:T(8,128)(2,1)} %get-tuple-element.19), calls=%async_computation | async-start | bytes 2359296 | tf_op jit(solution)/shard_map/all_to_all | solution.py:777
  61.4 1.0 copy-start
  138.9 32.9 %all-to-all-start.1 = ((bf16[32,128,128]{2,1,0:T(8,128)(2,1)}), bf16[32,128,128]{2,1,0:T(8,128)(2,1)S(1)}, u32[]{:S(2)}, u32[]{:S(2)}) async-start(bf16[32,128,128]{2,1,0:T(8,128)(2,1)} %collect.1), calls=%async_computation.1 | async-start | bytes 2097152 | tf_op jit(solution)/shard_map/all_to_all | solution.py:788
  171.8 1.0 copy-start.1
  197.4 41.1 %copy-start.2 = (f32[16,128,128]{2,1,0:T(8,128)S(1)}, f32[16,128,128]{2,1,0:T(8,128)}, u32[]{:S(2)}) copy-start(f32[16,128,128]{2,1,0:T(8,128)} %get-tuple-element.36) | copy-start | bytes 3145732
  238.4 1.0 copy-start.3
  238.4 1.7 copy-start.4
